TPU v7x, 512 devices: a whole 4x8x8 slice. The times are simulated.
512 devices in a mesh: doc: 32 (over x, y), leaf: 16 (over z, core).
Axes of the slice: x: 4, y: 8, z: 8, core: 2. Of those that a mesh axis runs over, the one named last changes fastest.
Arguments:
- docs: bfloat16 [16384, 768], P('doc', 'leaf'), may hold values from -6 to 6
- centroids: bfloat16 [32768, 768], P('leaf', 'doc'), may hold values from -6 to 6
Outputs:
- residual_rows: bfloat16 [16384, 768], P('doc', 'leaf')
- leaf_means: bfloat16 [32768, 768], P('leaf', 'doc')
All inputs are finite; a program needn't handle non-finite values.
Results may differ from a plain program's by a relative error of at most 0.015.
Values may be sent and summed in bfloat16 or wider, within the bound.
A program may use at most 64 MiB of HBM per device.

v0:
```python
import jax
import jax.numpy as jnp
from jax import lax
from jax.sharding import PartitionSpec as P


def body(docs, centroids):
    document_row_block = lax.all_gather(docs, "leaf", axis=1, tiled=True)
    leaf_row_block = lax.all_gather(centroids, "doc", axis=1, tiled=True)
    width = document_row_block.shape[1]
    input_single_float = document_row_block.astype(jnp.float32)
    approximate_input = (
        input_single_float
        / jnp.sqrt(jnp.mean(input_single_float * input_single_float, axis=1, keepdims=True) + 1e-06)
    ).astype(jnp.bfloat16)
    c32 = leaf_row_block.astype(jnp.float32)
    cnorm = jnp.sqrt(jnp.mean(c32 * c32, axis=1) + 1e-06)
    match_scores = lax.dot_general(
        approximate_input,
        leaf_row_block,
        (((1,), (1,)), ((), ())),
        preferred_element_type=jnp.float32,
    )
    kernel = jnp.exp(match_scores / (width * 0.02 * cnorm)[None, :])
    doc_count = document_row_block.shape[0] * lax.axis_size("doc")
    leaf_count = leaf_row_block.shape[0] * lax.axis_size("leaf")
    ratio = doc_count / leaf_count
    scales_v = jnp.ones((leaf_row_block.shape[0],), jnp.float32)
    scales_u = jnp.ones((document_row_block.shape[0],), jnp.float32)
    for step in range(2):
        row_portion = jnp.dot(kernel, scales_v, precision=lax.Precision.HIGHEST)
        scales_u = 1.0 / lax.psum(row_portion, "leaf")
        column_portion = jnp.dot(scales_u, kernel, precision=lax.Precision.HIGHEST)
        scales_v = ratio / lax.psum(column_portion, "doc")
    plan = (scales_u[:, None] * kernel * scales_v[None, :]).astype(jnp.bfloat16)
    recon_part = jnp.dot(plan, leaf_row_block, preferred_element_type=jnp.float32)
    recon = lax.psum_scatter(
        recon_part.astype(jnp.bfloat16), "leaf", scatter_dimension=1, tiled=True
    ).astype(jnp.float32)
    residual_rows = (docs.astype(jnp.float32) - recon).astype(jnp.bfloat16)
    sums_part = lax.dot_general(
        plan, document_row_block, (((0,), (0,)), ((), ())), preferred_element_type=jnp.float32
    )
    sums = lax.psum_scatter(
        sums_part.astype(jnp.bfloat16), "doc", scatter_dimension=1, tiled=True
    ).astype(jnp.float32)
    leaf_means = (sums * (leaf_count / doc_count)).astype(jnp.bfloat16)
    return (residual_rows, leaf_means)


def solution(mesh):
    return jax.shard_map(
        body,
        mesh=mesh,
        in_specs=(P("doc", "leaf"), P("leaf", "doc")),
        out_specs=(P("doc", "leaf"), P("leaf", "doc")),
        check_vma=False,
    )
```

profile of v0, /device:TPU:1, one launch (start us, length us, event | category | flops | bytes accessed | tf_op | source)
XLA Modules:
  0.0 610.1 jit_solution(16875571354013180341)
XLA Ops:
  7.2 0.0 all-gather.2.cloned.1.call-start
  7.2 0.7 all-gather.2.cloned.1.call-update
  7.9 0.0 reduce-scatter.3.cloned.1.call-start
  7.9 26.9 %all_gather.6 = bf16[512,768]{0,1:T(8,128)(2,1)S(1)} all-gather(bf16[512,48]{0,1:T(8,128)(2,1)} %param.2), channel_id=1, replica_groups=mesh['doc'=32,'leaf'=16] {'leaf'}, dimensions={1}, use_global_device_ids=true | all-gather | bytes 835584 | tf_op jit(solution)/shard_map/all_gather | solution.py:8
  34.9 0.2 fusion
  35.1 63.2 %all-gather.2.cloned.1.call-done = bf16[2048,768]{0,1:T(8,128)(2,1)} async-done(((bf16[2048,24]{0,1:T(8,128)(2,1)}), bf16[2048,768]{0,1:T(8,128)(2,1)}) %all-gather.2.cloned.1.call-update) | async-done | bytes 3145744 | tf_op jit(solution)/shard_map/all_gather | solution.py:9
  98.3 2.6 multiply_reduce_fusion
  100.8 3.8 divide_exponential_fusion
  104.7 1.9 copy-done
  106.6 3.6 fusion.4
  110.2 28.3 %psum.28 = f32[512]{0:T(512)S(1)} all-reduce(f32[512]{0:T(512)S(1)} %bitcast.23), channel_id=1, replica_groups=mesh['doc'=32,'leaf'=16] {'leaf'}, use_global_device_ids=true, to_apply=%region_2.0 | all-reduce | flops 512 | bytes 4096 | tf_op jit(solution)/shard_map/psum | solution.py:32
  138.5 4.3 fusion.7
  142.8 59.4 %psum.29 = f32[2048]{0:T(1024)S(1)} all-reduce(f32[2048]{0:T(1024)S(1)} %bitcast.17), channel_id=1, replica_groups=mesh['doc'=32,'leaf'=16] {'doc'}, use_global_device_ids=true, to_apply=%region_3.0 | all-reduce | flops 2048 | bytes 16384 | tf_op jit(solution)/shard_map/psum | solution.py:34
  202.2 5.9 fusion.8
  208.1 36.9 %psum.30 = f32[512]{0:T(512)S(1)} all-reduce(f32[512]{0:T(512)S(1)} %bitcast.22), channel_id=1, replica_groups=mesh['doc'=32,'leaf'=16] {'leaf'}, use_global_device_ids=true, to_apply=%region_4.0 | all-reduce | flops 512 | bytes 4096 | tf_op jit(solution)/shard_map/psum | solution.py:32
  245.1 4.3 fusion.9
  249.3 57.2 %psum.31 = f32[2048]{0:T(1024)S(1)} all-reduce(f32[2048]{0:T(1024)S(1)} %bitcast.19), channel_id=1, replica_groups=mesh['doc'=32,'leaf'=16] {'doc'}, use_global_device_ids=true, to_apply=%region_5.0 | all-reduce | flops 2048 | bytes 16384 | tf_op jit(solution)/shard_map/psum | solution.py:34
  306.6 5.0 convolution_convert_fusion.1
  311.6 0.0 reduce-scatter.5.cloned.1.call-start
  311.6 6.0 convolution_convert_fusion
  317.6 59.9 %reduce-scatter.3.cloned.1.call-done = bf16[512,48]{0,1:T(8,128)(2,1)} async-done(((bf16[512,768]{0,1:T(8,128)(2,1)}), bf16[512,48]{0,1:T(8,128)(2,1)}) %reduce-scatter.3.cloned.1.call-update) | async-done | bytes 49168 | tf_op jit(solution)/shard_map/reduce_scatter | solution.py:37
  377.6 1.4 subtract_convert_fusion
  379.0 223.0 %reduce-scatter.5.cloned.1.call-done = bf16[2048,24]{0,1:T(8,128)(2,1)} async-done(((bf16[2048,768]{0,1:T(8,128)(2,1)}), bf16[2048,24]{0,1:T(8,128)(2,1)}) %reduce-scatter.5.cloned.1.call-update) | async-done | bytes 98320 | tf_op jit(solution)/shard_map/reduce_scatter | solution.py:44
  602.0 1.6 multiply_convert_fusion.1
  (15 shorter events, 0.1 us)
Async XLA Ops:
  7.2 91.1 %all-gather.2.cloned.1.call-start = ((), (), s32[]{:S(2)}) async-start(), calls=%async_computation.2 | async-start | bytes 3244032 | tf_op jit(solution)/shard_map/all_gather | solution.py:9
  7.9 369.7 %reduce-scatter.3.cloned.1.call-start = ((), (), s32[]{:S(2)}) async-start(), calls=%async_computation.3 | async-start | bytes 835584 | tf_op jit(solution)/shard_map/reduce_scatter | solution.py:37
  34.8 69.8 %copy-start.2 = (bf16[512,768]{0,1:T(8,128)(2,1)}, bf16[512,768]{0,1:T(8,128)(2,1)S(1)}, u32[]{:S(2)}) copy-start(bf16[512,768]{0,1:T(8,128)(2,1)S(1)} %all_gather.6) | copy-start | bytes 2359300
  104.7 1.9 copy-start
  202.2 104.4 %copy-start.1 = (bf16[2048,768]{0,1:T(8,128)(2,1)S(1)}, bf16[2048,768]{0,1:T(8,128)(2,1)}, u32[]{:S(2)}) copy-start(bf16[2048,768]{0,1:T(8,128)(2,1)} %all-gather.2.cloned.1.call-done) | copy-start | bytes 9437188
  311.5 66.0 %copy-start.3 = (bf16[512,48]{0,1:T(8,128)(2,1)S(1)}, bf16[512,48]{0,1:T(8,128)(2,1)}, u32[]{:S(2)}) copy-start(bf16[512,48]{0,1:T(8,128)(2,1)} %param.2) | copy-start | bytes 147460
  311.6 290.5 %reduce-scatter.5.cloned.1.call-start = ((), (), s32[]{:S(2)}) async-start(), calls=%async_computation.4 | async-start | bytes 3244032 | tf_op jit(solution)/shard_map/reduce_scatter | solution.py:44
Sparse Core Ops, SparseCore 0:
  11.2 87.0 all-gather.1
  311.7 65.8 reduce-scatter.2
  382.7 219.3 reduce-scatter.4
where the time goes:
time: 614 us; the launch traced here: 610 us
  waiting for transfers between devices  347 us (57%)
  blocking collectives  209 us (34%)
  matrix products  32.9 us (5%)
  between operations  13.8 us (2%)
    reduce_scatter x1, waiting for transfers between devices, body(): lax.psum_scatter(sums_part.astype(jnp.bfloat16), 'doc', scatter_dimension...  223 us
    psum x2, blocking collectives, body(): scales_v = ratio / lax.psum(column_portion, 'doc')  117 us
    psum x2, blocking collectives, body(): scales_u = 1.0 / lax.psum(row_portion, 'leaf')  65.2 us
    all_gather x1, waiting for transfers between devices, body(): leaf_row_block = lax.all_gather(centroids, 'doc', axis=1, tiled=True)  63.2 us
    reduce_scatter x1, waiting for transfers between devices, body(): lax.psum_scatter(recon_part.astype(jnp.bfloat16), 'leaf', scatter_dimensi...  59.9 us
    all_gather x1, blocking collectives, body(): document_row_block = lax.all_gather(docs, 'leaf', axis=1, tiled=True)  26.9 us
  transfers between devices with their start and end apart: 3, of which 3 were waited for; matrix products, arithmetic and copies ran while one was open for 1% of the time, Pallas kernels for 0%

commit v1 on v0

v1 whole, which is shorter than its diff:
```python
import jax
import jax.numpy as jnp
from jax import lax
from jax.experimental import pallas as pl
from jax.experimental.pallas import tpu as pltpu
from jax.sharding import PartitionSpec as P

MESH = pl.DeviceIdType.MESH
F32 = jnp.float32
BF16 = jnp.bfloat16

E = 768
NX, NY, NZ, NL = 4, 8, 8, 16
FD, FL = 24, 48
ND, NV = 512, 2048
Q = 512
RATIO = 0.5

YSEQ = (0, -1, 1, -2, 2, -3, 3, -4)
XSEQ = (0, -1, 1, 2)


def kernel(
    docs_ref, cent_ref, res_ref, means_ref,
    dg, ca, cb, ct, xn, dt, kk, ww, ss, rr, ub, pbuf, ybuf, xbuf,
    gs, oa, ob, ra1, ra2, ray, rby, rbx, qq, rq, hq, sq, vv,
    d_send, d_recv, f_send, f_recv,
    ay_send, ay_recv, ax_send, ax_recv, af_send, af_recv,
    bx_send, bx_recv, by_send, by_recv,
    p_send, p_recv, y_send, y_recv, x_send, x_recv,
    rb_send, rb_recv, rbx_send, rbx_recv,
    ra1_send, ra1_recv, ra2_send, ra2_recv, ray_send, ray_recv,
    q1_send, q1_recv, q2_send, q2_recv,
):
    d = lax.axis_index("doc")
    l = lax.axis_index("leaf")
    x, y = lax.div(d, NY), lax.rem(d, NY)
    z, c = lax.div(l, 2), lax.rem(l, 2)

    def at_x(o):
        return lax.rem(x + o + NX, NX)

    def at_y(o):
        return lax.rem(y + o + NY, NY)

    def dev(ox, oy):
        return (at_x(ox) * NY + at_y(oy), l)

    def dev_leaf(zz, cc):
        return (d, zz * 2 + cc)

    other = dev_leaf(z, 1 - c)

    def copy(src, dst, s, r, to):
        return pltpu.make_async_remote_copy(
            src_ref=src, dst_ref=dst, send_sem=s, recv_sem=r, device_id=to, device_id_type=MESH
        )

    def took(ref, sem):
        pltpu.make_async_copy(ref, ref, sem).wait()

    barrier = pltpu.get_barrier_semaphore()

    def greet(to):
        pl.semaphore_signal(barrier, inc=1, device_id=to, device_id_type=MESH)

    def greet_leaf(i, _):
        greet((d, lax.rem(l + i, NL)))
        return 0

    def greet_y(i, _):
        greet((x * NY + lax.rem(y + i, NY), l))
        return 0

    def greet_x(i, _):
        greet((lax.rem(x + i, NX) * NY + y, l))
        return 0

    lax.fori_loop(1, NL, greet_leaf, 0)
    lax.fori_loop(1, NY, greet_y, 0)
    lax.fori_loop(1, NX, greet_x, 0)

    c32 = cent_ref[...].astype(F32)
    ca[x, y] = jnp.concatenate([c32[:, 0:Q], c32[:, Q:2 * Q]], axis=0).astype(BF16)
    cb[y, x] = jnp.concatenate([c32[:, 2 * Q:3 * Q], c32[:, 3 * Q:4 * Q]], axis=0).astype(BF16)
    dg[z, c] = docs_ref[...]

    pl.semaphore_wait(barrier, NL - 1 + NY - 1 + NX - 1)

    def ay(way, step, o):
        ref = ca.at[x, at_y(o)]
        return copy(ref, ref, ay_send.at[way, step], ay_recv.at[way, step], dev(0, 1 if way == 0 else -1))

    def ax(k, way, ox=0):
        ref = ca.at[at_x(ox), at_y(YSEQ[k])]
        return copy(ref, ref, ax_send.at[k, way], ax_recv.at[k, way], dev(1 if way == 0 else -1, 0))

    def af(k, ox):
        ref = ca.at[at_x(ox), at_y(YSEQ[k])]
        return copy(ref, ref, af_send.at[k], af_recv.at[k], dev(1 if k % 2 == 0 else -1, 0))

    def bx(m, ox):
        ref = cb.at[y, at_x(ox)]
        return copy(ref, ref, bx_send.at[m], bx_recv.at[m], dev(-1 if m == 1 else 1, 0))

    def by(way, step, m, o):
        ref = cb.at[at_y(o), at_x(XSEQ[m])]
        return copy(
            ref, ref, by_send.at[way, step, m], by_recv.at[way, step, m], dev(0, 1 if way == 0 else -1)
        )

    def start_ax(k):
        ax(k, 0).start()
        ax(k, 1).start()

    def start_by(m):
        by(0, 0, m, 0).start()
        by(1, 0, m, 0).start()

    def step_ay(s):
        ay(0, s - 1, -s).wait_recv()
        if s < 4:
            ay(0, s, -s).start()
        start_ax(YSEQ.index(-s))
        if s < 4:
            ay(1, s - 1, s).wait_recv()
            if s < 3:
                ay(1, s, s).start()
            start_ax(YSEQ.index(s))

    def step_by(s):
        for m in range(4):
            if s < 4 or m < 2:
                by(0, s - 1, m, -s).wait_recv()
                if s < 3 or (s == 3 and m < 2):
                    by(0, s, m, -s).start()
            if s < 4 or m >= 2:
                by(1, s - 1, m, s).wait_recv()
                if s < 3 or (s == 3 and m >= 2):
                    by(1, s, m, s).start()

    def step_ax(k):
        ax(k, 0, -1).wait_recv()
        if k % 2 == 0:
            af(k, -1).start()
        ax(k, 1, 1).wait_recv()
        if k % 2 == 1:
            af(k, 1).start()

    ay(0, 0, 0).start()
    ay(1, 0, 0).start()
    start_ax(0)
    bx(0, 0).start()
    bx(1, 0).start()
    start_by(0)

    def send_docs(i, _):
        zz = lax.rem(z + i, NZ)
        copy(dg.at[z, c], dg.at[z, c], d_send, d_recv.at[NZ - i], dev_leaf(zz, c)).start()
        return 0

    lax.fori_loop(1, NZ, send_docs, 0)
    copy(dg.at[z, c], dg.at[z, c], f_send, f_recv, other).start()

    step_ay(1)
    bx(0, -1).wait_recv()
    bx(2, -1).start()
    start_by(1)
    bx(1, 1).wait_recv()
    start_by(2)
    step_ay(2)
    bx(2, 2).wait_recv()
    start_by(3)
    step_ax(0)
    step_by(1)
    step_ay(3)
    step_ax(1)
    step_ax(2)
    step_by(2)
    step_ay(4)
    step_ax(3)
    step_ax(4)

    def pass_docs(i, _):
        zz = lax.rem(z + i, NZ)
        ref = dg.at[zz, c]
        copy(ref, ref, d_send, d_recv.at[i], other).wait_recv()
        copy(ref, ref, f_send, f_recv, other).start()
        return 0

    lax.fori_loop(1, NZ, pass_docs, 0)
    step_by(3)
    for k in range(5, 8):
        step_ax(k)
    step_by(4)
    for k in range(8):
        af(k, 2).wait_recv()
    took(dg.at[:, 0], f_recv)

    dt[...] = dg[...].reshape(E, ND)
    for j in range(4):
        block = dt[:, pl.ds(128 * j, 128)].astype(F32)
        scale = 1.0 / jnp.sqrt(jnp.sum(block * block, axis=0, keepdims=True) * (1.0 / E) + 1e-06)
        xn[pl.ds(128 * j, 128), :] = (block * scale).T.astype(BF16)

    ss[...] = jnp.zeros_like(ss)

    def unpack(t, _):
        xx, yy = lax.div(t, 4), 2 * lax.rem(t, 4)
        rows = pl.ds(pl.multiple_of(t * FL, FL), FL)
        for h in range(2):
            if h == 0:
                u0, u1 = ca[xx, yy].astype(F32), ca[xx, yy + 1].astype(F32)
            else:
                u0, u1 = cb[yy, xx].astype(F32), cb[yy + 1, xx].astype(F32)
            for g in range(2):
                part = jnp.concatenate([u0[FD * g:FD * g + FD], u1[FD * g:FD * g + FD]], axis=0)
                cols = pl.ds((2 * h + g) * Q, Q)
                ct[rows, cols] = part.astype(BF16)
                ss[:, cols] += jnp.sum((part * part).reshape(FL // 8, 8, Q), axis=0)
        return 0

    lax.fori_loop(0, NL, unpack, 0)

    rr[...] = jnp.zeros_like(rr)
    T = 256

    def scores(n, _):
        cols = pl.ds(pl.multiple_of(n * T, T), T)
        norm = jnp.sqrt(jnp.sum(ss[:, cols], axis=0, keepdims=True) * (1.0 / E) + 1e-06)
        s = jnp.dot(xn[...], ct[:, cols], preferred_element_type=F32)
        k = jnp.exp(s * (1.0 / (E * 0.02 * norm)))
        kk[:, cols] = k
        rr[...] += k[:, 0:128] + k[:, 128:256]
        return 0

    lax.fori_loop(0, NV // T, scores, 0)

    def reduce_leaf(i):
        pbuf[i, l] = jnp.sum(rr[...].T, axis=0, keepdims=True)

        def send(j, _):
            copy(
                pbuf.at[i, l], pbuf.at[i, l], p_send.at[i], p_recv.at[i], (d, lax.rem(l + j, NL))
            ).start()
            return 0

        lax.fori_loop(1, NL, send, 0)
        took(pbuf.at[i, pl.ds(0, NL - 1)], p_recv.at[i])
        u = 1.0 / jnp.sum(pbuf[i], axis=0)
        ub[...] = jnp.broadcast_to(u, (128, ND)).T

    def columns(i):
        def one(n, _):
            cols = pl.ds(pl.multiple_of(n * 128, 128), 128)
            w = kk[:, cols] * ub[...]
            if i == 1:
                ww[:, cols] = w.astype(BF16)
            ybuf[i, y, :, cols] = jnp.sum(jnp.sum(w.reshape(ND // 8, 8, 128), axis=0), axis=0, keepdims=True)
            return 0

        lax.fori_loop(0, NV // 128, one, 0)

    def send_y(i):
        def send(j, _):
            to = (x * NY + lax.rem(y + j, NY), l)
            copy(ybuf.at[i, y], ybuf.at[i, y], y_send.at[i], y_recv.at[i], to).start()
            return 0

        lax.fori_loop(1, NY, send, 0)

    def send_x(i):
        took(ybuf.at[i, pl.ds(0, NY - 1)], y_recv.at[i])
        xbuf[i, x] = jnp.sum(ybuf[i], axis=0)

        def send(j, _):
            to = (lax.rem(x + j, NX) * NY + y, l)
            copy(xbuf.at[i, x], xbuf.at[i, x], x_send.at[i], x_recv.at[i], to).start()
            return 0

        lax.fori_loop(1, NX, send, 0)

    def take_x(i):
        took(xbuf.at[i, pl.ds(0, NX - 1)], x_recv.at[i])
        vv[...] = RATIO / jnp.sum(xbuf[i], axis=0)

    reduce_leaf(0)
    columns(0)
    send_y(0)
    send_x(0)
    take_x(0)

    rr[...] = jnp.zeros_like(rr)

    def rows_of(n, _):
        cols = pl.ds(pl.multiple_of(n * 128, 128), 128)
        rr[...] += kk[:, cols] * vv[:, cols]
        return 0

    lax.fori_loop(0, NV // 128, rows_of, 0)
    reduce_leaf(1)
    columns(1)
    send_y(1)

    def products(h):
        def one(xx, _):
            rows = pl.ds(pl.multiple_of(xx * 192, 192), 192)
            gs[...] = jnp.dot(dt[rows, :], ww[:, 2 * Q * h:2 * Q * (h + 1)], preferred_element_type=F32)
            for yy in range(NY):
                unit = jnp.concatenate(
                    [gs[FD * yy:FD * yy + FD, 0:Q], gs[FD * yy:FD * yy + FD, Q:2 * Q]], axis=0
                ).astype(BF16)
                if h == 0:
                    oa[xx, yy] = unit
                else:
                    ob[yy, xx] = unit
            return 0

        lax.fori_loop(0, NX, one, 0)

    def rb(way, step, m):
        o = (4 - step) if way == 0 else (step - 4)
        return copy(
            ob.at[at_y(o), at_x(XSEQ[m])], rby.at[way, step, m],
            rb_send.at[way, step, m], rb_recv.at[way, step, m], dev(0, 1 if way == 0 else -1),
        )

    def step_rb(s):
        for way in range(2):
            o = (4 - s) if way == 0 else (s - 4)
            for m in range(4):
                ref = ob.at[at_y(o), at_x(XSEQ[m])]
                if s > 1 or (m < 2 if way == 0 else m >= 2):
                    rb(way, s - 1, m).wait_recv()
                    ref[...] = (ref[...].astype(F32) + rby[way, s - 1, m].astype(F32)).astype(BF16)
                if s < 4:
                    rb(way, s, m).start()

    def ra_first(k):
        yy = at_y(YSEQ[k])
        way = k % 2
        return copy(
            oa.at[at_x(2), yy], ra1.at[k], ra1_send.at[k], ra1_recv.at[k], dev(1 if way == 0 else -1, 0)
        )

    def ra_second(k, way):
        o = 1 if way == 0 else -1
        return copy(
            oa.at[at_x(o), at_y(YSEQ[k])], ra2.at[way, k], ra2_send.at[way, k], ra2_recv.at[way, k], dev(o, 0)
        )

    def ra_last(k):
        o = YSEQ[k]
        return copy(oa.at[x, at_y(o)], ray.at[k], ray_send, ray_recv, dev(0, o))

    products(1)
    for m in range(2):
        rb(0, 0, m).start()
        rb(1, 0, m + 2).start()
    products(0)
    KSEQ = (7, 5, 6, 3, 4, 1, 2, 0)
    for k in KSEQ:
        ra_first(k).start()
    for k in KSEQ:
        ra_second(k, 1 - k % 2).start()
    send_x(1)
    step_rb(1)
    for k in KSEQ:
        way = k % 2
        ra_first(k).wait_recv()
        ref = oa.at[at_x(1 if way == 0 else -1), at_y(YSEQ[k])]
        ref[...] = (ref[...].astype(F32) + ra1[k].astype(F32)).astype(BF16)
        ra_second(k, way).start()
    take_x(1)

    def weigh(n, _):
        cols = pl.ds(pl.multiple_of(n * 128, 128), 128)
        ww[:, cols] = (kk[:, cols] * ub[...] * vv[:, cols]).astype(BF16)
        return 0

    lax.fori_loop(0, NV // 128, weigh, 0)

    def recon(t, _):
        rows = pl.ds(pl.multiple_of(t * 2 * FL, 2 * FL), 2 * FL)
        part = lax.dot_general(ct[rows, :], ww[...], (((1,), (1,)), ((), ())), preferred_element_type=F32)
        qq[0, t] = part[0:FL].astype(BF16)
        qq[1, t] = part[FL:2 * FL].astype(BF16)
        return 0

    lax.fori_loop(0, NZ, recon, 0)
    first = copy(qq.at[1 - c], rq, q1_send, q1_recv, other)
    first.start()

    step_rb(2)

    first.wait_recv()

    def add_other(t, _):
        hq[t] = (qq[c, t].astype(F32) + rq[t].astype(F32)).astype(BF16)
        return 0

    lax.fori_loop(0, NZ, add_other, 0)

    def send_recon(i, _):
        zz = lax.rem(z + i, NZ)
        copy(hq.at[zz], sq.at[i], q2_send, q2_recv, dev_leaf(zz, c)).start()
        return 0

    lax.fori_loop(1, NZ, send_recon, 0)

    step_rb(3)
    for k in KSEQ:
        ref = oa.at[x, at_y(YSEQ[k])]
        ra_second(k, 0).wait_recv()
        ra_second(k, 1).wait_recv()
        ref[...] = (ref[...].astype(F32) + ra2[0, k].astype(F32) + ra2[1, k].astype(F32)).astype(BF16)
        if k:
            ra_last(k).start()
    step_rb(4)

    def rbx_copy(m):
        return copy(ob.at[y, at_x(XSEQ[m])], rbx.at[m], rbx_send, rbx_recv, dev(XSEQ[m], 0))

    for m in range(1, 4):
        rbx_copy(m).start()

    took(sq.at[pl.ds(1, NZ - 1)], q2_recv)
    back = hq[z].astype(F32)
    for i in range(1, NZ):
        back = back + sq[i].astype(F32)
    res_ref[...] = (docs_ref[...].astype(F32) - back).astype(BF16)

    v = vv[...] * (1.0 / RATIO)
    took(rbx.at[pl.ds(1, 3)], rbx_recv)
    total = ob[y, x].astype(F32)
    for m in range(1, 4):
        total = total + rbx[m].astype(F32)
    means_ref[:, 2 * Q:3 * Q] = (total[0:FD] * v[:, 2 * Q:3 * Q]).astype(BF16)
    means_ref[:, 3 * Q:4 * Q] = (total[FD:2 * FD] * v[:, 3 * Q:4 * Q]).astype(BF16)

    took(ray.at[pl.ds(1, NY - 1)], ray_recv)
    total = oa[x, y].astype(F32)
    for k in range(1, NY):
        total = total + ray[k].astype(F32)
    means_ref[:, 0:Q] = (total[0:FD] * v[:, 0:Q]).astype(BF16)
    means_ref[:, Q:2 * Q] = (total[FD:2 * FD] * v[:, Q:2 * Q]).astype(BF16)

    took(dg.at[pl.ds(0, NZ - 1), 0], d_send)
    took(dg.at[:, 0], f_send)
    for s in range(4):
        ay(0, s, 0).wait_send()
        if s < 3:
            ay(1, s, 0).wait_send()
        for m in range(4):
            if s < 3 or m < 2:
                by(0, s, m, 0).wait_send()
            if s < 3 or m >= 2:
                by(1, s, m, 0).wait_send()
            if s > 0 or m < 2:
                rb(0, s, m).wait_send()
            if s > 0 or m >= 2:
                rb(1, s, m).wait_send()
    for k in range(8):
        ax(k, 0).wait_send()
        ax(k, 1).wait_send()
        af(k, 0).wait_send()
        ra_first(k).wait_send()
        ra_second(k, 0).wait_send()
        ra_second(k, 1).wait_send()
    for m in range(3):
        bx(m, 0).wait_send()
    for i in range(2):
        took(pbuf.at[i, pl.ds(0, NL - 1)], p_send.at[i])
        took(ybuf.at[i, pl.ds(0, NY - 1)], y_send.at[i])
        took(xbuf.at[i, pl.ds(0, NX - 1)], x_send.at[i])
    first.wait_send()
    took(sq.at[pl.ds(1, NZ - 1)], q2_send)
    took(rbx.at[pl.ds(1, 3)], rbx_send)
    took(ray.at[pl.ds(1, NY - 1)], ray_send)


def body(docs, centroids):
    dma = pltpu.SemaphoreType.DMA
    residual, means = pl.pallas_call(
        kernel,
        out_shape=(jax.ShapeDtypeStruct((FL, ND), BF16), jax.ShapeDtypeStruct((FD, NV), BF16)),
        in_specs=[pl.BlockSpec(memory_space=pltpu.VMEM)] * 2,
        out_specs=(pl.BlockSpec(memory_space=pltpu.VMEM),) * 2,
        scratch_shapes=[
            pltpu.VMEM((NZ, 2, FL, ND), BF16),
            pltpu.VMEM((NX, NY, 2 * FD, Q), BF16),
            pltpu.VMEM((NY, NX, 2 * FD, Q), BF16),
            pltpu.VMEM((E, NV), BF16),
            pltpu.VMEM((ND, E), BF16),
            pltpu.VMEM((E, ND), BF16),
            pltpu.VMEM((ND, NV), F32),
            pltpu.VMEM((ND, NV), BF16),
            pltpu.VMEM((8, NV), F32),
            pltpu.VMEM((ND, 128), F32),
            pltpu.VMEM((ND, 128), F32),
            pltpu.VMEM((2, NL, 1, ND), F32),
            pltpu.VMEM((2, NY, 1, NV), F32),
            pltpu.VMEM((2, NX, 1, NV), F32),
            pltpu.VMEM((192, 2 * Q), F32),
            pltpu.VMEM((NX, NY, 2 * FD, Q), BF16),
            pltpu.VMEM((NY, NX, 2 * FD, Q), BF16),
            pltpu.VMEM((8, 2 * FD, Q), BF16),
            pltpu.VMEM((2, 8, 2 * FD, Q), BF16),
            pltpu.VMEM((8, 2 * FD, Q), BF16),
            pltpu.VMEM((2, 4, 4, 2 * FD, Q), BF16),
            pltpu.VMEM((4, 2 * FD, Q), BF16),
            pltpu.VMEM((2, NZ, FL, ND), BF16),
            pltpu.VMEM((NZ, FL, ND), BF16),
            pltpu.VMEM((NZ, FL, ND), BF16),
            pltpu.VMEM((NZ, FL, ND), BF16),
            pltpu.VMEM((1, NV), F32),
            dma, dma((NZ,)), dma, dma,
            dma((2, 4)), dma((2, 4)), dma((8, 2)), dma((8, 2)), dma((8,)), dma((8,)),
            dma((3,)), dma((3,)), dma((2, 4, 4)), dma((2, 4, 4)),
            dma((2,)), dma((2,)), dma((2,)), dma((2,)), dma((2,)), dma((2,)),
            dma((2, 4, 4)), dma((2, 4, 4)), dma, dma,
            dma((8,)), dma((8,)), dma((2, 8)), dma((2, 8)), dma, dma,
            dma, dma, dma, dma,
        ],
        compiler_params=pltpu.CompilerParams(
            collective_id=0, has_side_effects=True, vmem_limit_bytes=48 * 2**20
        ),
        cost_estimate=pl.CostEstimate(
            flops=6 * ND * NV * E, bytes_accessed=2 * (ND * FL + NV * FD) * 2, transcendentals=ND * NV
        ),
    )(docs.T, centroids.T)
    return residual.T, means.T


def solution(mesh):
    return jax.shard_map(
        body,
        mesh=mesh,
        in_specs=(P("doc", "leaf"), P("leaf", "doc")),
        out_specs=(P("doc", "leaf"), P("leaf", "doc")),
        check_vma=False,
    )
```

time: 614 us -> 113 us (0.18)
  waiting for transfers between devices: 347 us -> 0 us
  blocking collectives: 209 us -> 0 us
  Pallas kernels: 0 us -> 108 us
  matrix products: 32.9 us -> 0 us
  between operations: 13.8 us -> 0.65 us
    reduce_scatter x2 -> x0, waiting for transfers between devices: 283 us -> none  [the longest x1 223 us: body(): lax.psum_scatter(sums_part.astype(jnp.bfloat16), 'doc', scatter_dimension...]
    psum x4 -> x0, blocking collectives: 182 us -> none  [the longest x2 117 us: body(): scales_v = ratio / lax.psum(column_portion, 'doc')]
    pallas_call x0 -> x1, Pallas kernels: none -> 108 us  [body(): pl.pallas_call(kernel, out_shape=(jax.ShapeDtypeStruct((FL, ND), BF16), j...]
    all_gather x1 -> x0, waiting for transfers between devices: 63.2 us -> none  [body(): leaf_row_block = lax.all_gather(centroids, 'doc', axis=1, tiled=True)]
    dot_general x7 -> x0, matrix products: 32.9 us -> none  [the longest x2 9.53 us: body(): row_portion = jnp.dot(kernel, scales_v, precision=lax.Precision.HIGHEST)]
    all_gather x1 -> x0, blocking collectives: 26.9 us -> none  [body(): document_row_block = lax.all_gather(docs, 'leaf', axis=1, tiled=True)]
  transfers between devices with their start and end apart: 3 -> 0, of which waited for: 3 -> 0; matrix products, arithmetic and copies ran while one was open for 1% -> 0% of each run, Pallas kernels for 0% -> 0%
where the time goes in v1:
time: 113 us; the launch traced here: 112 us
  Pallas kernels  108 us (96%)
  local copies, waits for them, and re-layouts  2.95 us (3%)
    pallas_call x1, Pallas kernels, body(): pl.pallas_call(kernel, out_shape=(jax.ShapeDtypeStruct((FL, ND), BF16), j...  108 us
    unnamed x6, local copies, waits for them, and re-layouts  2.95 us

profile of v1, /device:TPU:1, one launch (start us, length us, event | category | flops | bytes accessed | tf_op | source)
XLA Modules:
  0.0 111.7 jit_solution(16339873995296079046)
XLA Ops:
  0.6 0.0 copy-start
  0.6 0.9 copy-done
  1.5 0.0 copy-start.1
  1.5 0.8 copy-done.1
  2.3 108.1 %shard_map.41 = (bf16[48,512]{1,0:T(8,128)(2,1)S(1)}, bf16[24,2048]{1,0:T(8,128)(2,1)S(1)}) custom-call(bf16[48,512]{1,0:T(8,128)(2,1)S(1)} %bitcast.7, bf16[24,2048]{1,0:T(8,128)(2,1)S(1)} %bitcast.6), custom_call_target="tpu_custom_call" | custom-call | flops 4831838208 | bytes 294912 | tf_op jit(solution)/shard_map/pallas_call | solution.py:484
  110.4 0.6 copy.6
  111.0 0.6 copy.7
Async XLA Ops:
  0.6 0.9 copy-start
  1.5 0.8 copy-start.1

commit v2 on v1

v2 whole, which is shorter than its diff:
```python
import jax
import jax.numpy as jnp
from jax import lax
from jax.experimental import pallas as pl
from jax.experimental.pallas import tpu as pltpu
from jax.sharding import PartitionSpec as P

MESH = pl.DeviceIdType.MESH
F32 = jnp.float32
BF16 = jnp.bfloat16

E = 768
NX, NY, NZ, NL = 4, 8, 8, 16
FD, FL = 24, 48
ND, NV = 512, 2048
QA, QB = 640, 384
COLS = ((0, QA), (QA, QA), (2 * QA, QB), (2 * QA + QB, QB))
RATIO = 0.5

YSEQ = (0, -1, 1, -2, 2, -3, 3, -4)
XSEQ = (0, -1, 1, 2)
HOPS = ((1, 0), (-1, 0), (2, 0), (-2, 0), (1, -2), (-1, 2), (2, -2))
BACK = ((1, 1), (-1, -1), (2, 2), (-2, -2), (1, 3), (-1, -3), (2, 4))


def kernel(
    docs_hbm, cent_hbm, res_ref, means_ref,
    docs_ref, cent_ref, in_sem, dg, ca, cb, ct, xn, dt, kk, ww, ss, rr, ub, pbuf, ybuf, xbuf,
    gs, oa, ob, ra1, ra2, ray, rby, rbx, qq, rq, sq, vv,
    d_send, d_recv, f_send, f_recv,
    ay_send, ay_recv, ax_send, ax_recv, af_send, af_recv,
    bx_send, bx_recv, by_send, by_recv,
    p_send, p_recv, y_send, y_recv, x_send, x_recv,
    rb_send, rb_recv, rbx_send, rbx_recv,
    ra1_send, ra1_recv, ra2_send, ra2_recv, ray_send, ray_recv,
    q1_send, q1_recv, q2_send, q2_recv,
):
    d = lax.axis_index("doc")
    l = lax.axis_index("leaf")
    x, y = lax.div(d, NY), lax.rem(d, NY)
    z, c = lax.div(l, 2), lax.rem(l, 2)

    def at_x(o):
        return lax.rem(x + o + NX, NX)

    def at_y(o):
        return lax.rem(y + o + NY, NY)

    def at_z(o):
        return lax.rem(z + o + NZ, NZ)

    def dev(ox, oy):
        return (at_x(ox) * NY + at_y(oy), l)

    def dev_leaf(zz, cc):
        return (d, zz * 2 + cc)

    other = dev_leaf(z, 1 - c)

    def copy(src, dst, s, r, to):
        return pltpu.make_async_remote_copy(
            src_ref=src, dst_ref=dst, send_sem=s, recv_sem=r, device_id=to, device_id_type=MESH
        )

    def took(ref, sem):
        pltpu.make_async_copy(ref, ref, sem).wait()

    into = (
        pltpu.make_async_copy(cent_hbm, cent_ref, in_sem.at[0]),
        pltpu.make_async_copy(docs_hbm, docs_ref, in_sem.at[1]),
    )
    for one in into:
        one.start()

    barrier = pltpu.get_barrier_semaphore()

    def greet(to):
        pl.semaphore_signal(barrier, inc=1, device_id=to, device_id_type=MESH)

    def greet_leaf(i, _):
        greet((d, lax.rem(l + i, NL)))
        return 0

    def greet_y(i, _):
        greet((x * NY + lax.rem(y + i, NY), l))
        return 0

    def greet_x(i, _):
        greet((lax.rem(x + i, NX) * NY + y, l))
        return 0

    lax.fori_loop(1, NL, greet_leaf, 0)
    lax.fori_loop(1, NY, greet_y, 0)
    lax.fori_loop(1, NX, greet_x, 0)

    for one in into:
        one.wait()
    c32 = cent_ref[...].astype(F32)
    own = [c32[:, at:at + n] for at, n in COLS]
    ca[x, y] = jnp.concatenate(own[0:2], axis=0).astype(BF16)
    cb[y, x] = jnp.concatenate(own[2:4], axis=0).astype(BF16)
    dg[z, c] = docs_ref[...]

    pl.semaphore_wait(barrier, NL - 1 + NY - 1 + NX - 1)

    def ay(i):
        to, o = HOPS[i]
        ref = ca.at[x, at_y(o)]
        return copy(ref, ref, ay_send.at[i], ay_recv.at[i], dev(0, to))

    def ax(k, way, ox=0):
        ref = ca.at[at_x(ox), at_y(YSEQ[k])]
        return copy(ref, ref, ax_send.at[k, way], ax_recv.at[k, way], dev(1 if way == 0 else -1, 0))

    def af(k, ox):
        ref = ca.at[at_x(ox), at_y(YSEQ[k])]
        return copy(ref, ref, af_send.at[k], af_recv.at[k], dev(1 if k % 2 == 0 else -1, 0))

    def bx(i):
        ref = cb.at[y, x]
        return copy(ref, ref, bx_send.at[i], bx_recv.at[i], dev((1, -1, 2)[i], 0))

    def by(way, step, m, o):
        ref = cb.at[at_y(o), at_x(XSEQ[m])]
        return copy(
            ref, ref, by_send.at[way, step, m], by_recv.at[way, step, m], dev(0, 1 if way == 0 else -1)
        )

    def dz(i):
        to, o = HOPS[i]
        ref = dg.at[at_z(o), c]
        return copy(ref, ref, d_send.at[i], d_recv.at[i], dev_leaf(at_z(to), c))

    def pass_docs(o):
        ref = dg.at[at_z(o), c]
        copy(ref, ref, f_send, f_recv, other).start()

    def start_ax(k):
        ax(k, 0).start()
        ax(k, 1).start()

    def start_by(m):
        by(0, 0, m, 0).start()
        by(1, 0, m, 0).start()

    def step_ay(i):
        ay(i).wait_recv()
        if i == 2:
            ay(4).start()
            ay(6).start()
        if i == 3:
            ay(5).start()
        start_ax(i + 1)

    def step_dz(i):
        dz(i).wait_recv()
        if i == 2:
            dz(4).start()
            dz(6).start()
        if i == 3:
            dz(5).start()
        pass_docs(YSEQ[i + 1])

    def step_bx(i):
        bx(i).wait_recv()
        start_by(i + 1)

    def step_by(s, m):
        if s < 4:
            by(0, s - 1, m, -s).wait_recv()
            if s < 3:
                by(0, s, m, -s).start()
        by(1, s - 1, m, s).wait_recv()
        if s < 4:
            by(1, s, m, s).start()

    def step_ax(k):
        ax(k, 0, -1).wait_recv()
        if k % 2 == 0:
            af(k, -1).start()
        ax(k, 1, 1).wait_recv()
        if k % 2 == 1:
            af(k, 1).start()

    for i in range(4):
        ay(i).start()
    for i in range(3):
        bx(i).start()
    start_by(0)
    start_ax(0)
    for i in range(4):
        dz(i).start()
    pass_docs(0)

    step_ay(0)
    step_ay(1)
    step_bx(0)
    step_bx(1)
    step_ay(2)
    step_ay(3)
    step_by(1, 0)
    step_ax(0)
    step_bx(2)
    for i in range(4):
        step_dz(i)
    step_by(1, 1)
    step_by(1, 2)
    step_by(2, 0)
    step_ax(1)
    step_ax(2)
    for i in range(4, 7):
        step_ay(i)
    step_by(1, 3)
    step_by(2, 1)
    step_by(2, 2)
    step_ax(3)
    step_ax(4)
    step_by(3, 0)
    step_by(2, 3)
    for i in range(4, 7):
        step_dz(i)
    step_by(3, 1)
    step_ax(5)
    step_by(3, 2)
    step_ax(6)
    step_by(3, 3)
    step_by(4, 0)
    step_ax(7)
    for m in range(1, 4):
        step_by(4, m)
    for k in range(8):
        af(k, 2).wait_recv()
    took(dg.at[:, 0], f_recv)

    dt[...] = dg[...].reshape(E, ND)
    for j in range(4):
        block = dt[:, pl.ds(128 * j, 128)].astype(F32)
        scale = 1.0 / jnp.sqrt(jnp.sum(block * block, axis=0, keepdims=True) * (1.0 / E) + 1e-06)
        xn[pl.ds(128 * j, 128), :] = (block * scale).T.astype(BF16)

    ss[...] = jnp.zeros_like(ss)

    def unpack(t, _):
        xx, yy = lax.div(t, 4), 2 * lax.rem(t, 4)
        rows = pl.ds(pl.multiple_of(t * FL, FL), FL)
        for h in range(2):
            if h == 0:
                u0, u1 = ca[xx, yy].astype(F32), ca[xx, yy + 1].astype(F32)
            else:
                u0, u1 = cb[yy, xx].astype(F32), cb[yy + 1, xx].astype(F32)
            for g in range(2):
                part = jnp.concatenate([u0[FD * g:FD * g + FD], u1[FD * g:FD * g + FD]], axis=0)
                at, n = COLS[2 * h + g]
                cols = pl.ds(at, n)
                ct[rows, cols] = part.astype(BF16)
                ss[:, cols] += jnp.sum((part * part).reshape(FL // 8, 8, n), axis=0)
        return 0

    lax.fori_loop(0, NL, unpack, 0)

    rr[...] = jnp.zeros_like(rr)
    T = 256

    def scores(n, _):
        cols = pl.ds(pl.multiple_of(n * T, T), T)
        norm = jnp.sqrt(jnp.sum(ss[:, cols], axis=0, keepdims=True) * (1.0 / E) + 1e-06)
        s = jnp.dot(xn[...], ct[:, cols], preferred_element_type=F32)
        k = jnp.exp(s * (1.0 / (E * 0.02 * norm)))
        kk[:, cols] = k
        rr[...] += k[:, 0:128] + k[:, 128:256]
        return 0

    lax.fori_loop(0, NV // T, scores, 0)

    def reduce_leaf(i):
        pbuf[i, l] = jnp.sum(rr[...].T, axis=0, keepdims=True)

        def send(j, _):
            copy(
                pbuf.at[i, l], pbuf.at[i, l], p_send.at[i], p_recv.at[i], (d, lax.rem(l + j, NL))
            ).start()
            return 0

        lax.fori_loop(1, NL, send, 0)
        took(pbuf.at[i, pl.ds(0, NL - 1)], p_recv.at[i])
        u = 1.0 / jnp.sum(pbuf[i], axis=0)
        ub[...] = jnp.broadcast_to(u, (128, ND)).T

    def columns(i):
        def one(n, _):
            cols = pl.ds(pl.multiple_of(n * 128, 128), 128)
            w = kk[:, cols] * ub[...]
            if i == 1:
                ww[:, cols] = w.astype(BF16)
            ybuf[i, y, :, cols] = jnp.sum(jnp.sum(w.reshape(ND // 8, 8, 128), axis=0), axis=0, keepdims=True)
            return 0

        lax.fori_loop(0, NV // 128, one, 0)

    def send_y(i):
        def send(j, _):
            to = (x * NY + lax.rem(y + j, NY), l)
            copy(ybuf.at[i, y], ybuf.at[i, y], y_send.at[i], y_recv.at[i], to).start()
            return 0

        lax.fori_loop(1, NY, send, 0)

    def send_x(i):
        took(ybuf.at[i, pl.ds(0, NY - 1)], y_recv.at[i])
        xbuf[i, x] = jnp.sum(ybuf[i], axis=0)

        def send(j, _):
            to = (lax.rem(x + j, NX) * NY + y, l)
            copy(xbuf.at[i, x], xbuf.at[i, x], x_send.at[i], x_recv.at[i], to).start()
            return 0

        lax.fori_loop(1, NX, send, 0)

    def take_x(i):
        took(xbuf.at[i, pl.ds(0, NX - 1)], x_recv.at[i])
        vv[...] = RATIO / jnp.sum(xbuf[i], axis=0)

    reduce_leaf(0)
    columns(0)
    send_y(0)
    send_x(0)
    take_x(0)

    rr[...] = jnp.zeros_like(rr)

    def rows_of(n, _):
        cols = pl.ds(pl.multiple_of(n * 128, 128), 128)
        rr[...] += kk[:, cols] * vv[:, cols]
        return 0

    lax.fori_loop(0, NV // 128, rows_of, 0)
    reduce_leaf(1)
    columns(1)
    send_y(1)

    def products(h, xx):
        rows = pl.ds(pl.multiple_of(xx * 192, 192), 192)
        (a0, n0), (a1, n1) = COLS[2 * h], COLS[2 * h + 1]
        gs[:, 0:n0 + n1] = jnp.dot(dt[rows, :], ww[:, a0:a1 + n1], preferred_element_type=F32)
        for yy in range(NY):
            r = FD * yy
            unit = jnp.concatenate([gs[r:r + FD, 0:n0], gs[r:r + FD, n0:n0 + n1]], axis=0).astype(BF16)
            if h == 0:
                oa[xx, yy] = unit
            else:
                ob[yy, xx] = unit

    def add(ref, *others):
        total = ref[...].astype(F32)
        for one in others:
            total = total + one.astype(F32)
        ref[...] = total.astype(BF16)

    def rb(way, step, m):
        o = (3 - step) if way == 0 else (step - 4)
        return copy(
            ob.at[at_y(o), at_x(XSEQ[m])], rby.at[way, step, m],
            rb_send.at[way, step, m], rb_recv.at[way, step, m], dev(0, 1 if way == 0 else -1),
        )

    def step_rb(way, s, m):
        rb(way, s - 1, m).wait_recv()
        add(ob.at[at_y((3 - s) if way == 0 else (s - 4)), at_x(XSEQ[m])], rby[way, s - 1, m])
        if s < (3 if way == 0 else 4):
            rb(way, s, m).start()

    def rbx_copy(m):
        return copy(ob.at[y, at_x(XSEQ[m])], rbx.at[m], rbx_send, rbx_recv, dev(XSEQ[m], 0))

    def ra_first(k):
        way = k % 2
        return copy(
            oa.at[at_x(2), at_y(YSEQ[k])], ra1.at[k], ra1_send.at[k], ra1_recv.at[k],
            dev(1 if way == 0 else -1, 0),
        )

    def ra_second(k, way):
        o = 1 if way == 0 else -1
        return copy(
            oa.at[at_x(o), at_y(YSEQ[k])], ra2.at[way, k], ra2_send.at[way, k], ra2_recv.at[way, k], dev(o, 0)
        )

    def ra_last(i):
        to, o = BACK[i]
        return copy(oa.at[x, at_y(o)], ray.at[i], ray_send.at[i], ray_recv.at[i], dev(0, to))

    def step_ra1(k):
        ra_first(k).wait_recv()
        add(oa.at[at_x(1 if k % 2 == 0 else -1), at_y(YSEQ[k])], ra1[k])
        ra_second(k, k % 2).start()

    def step_ra2(k):
        ra_second(k, 0).wait_recv()
        ra_second(k, 1).wait_recv()
        add(oa.at[x, at_y(YSEQ[k])], ra2[0, k], ra2[1, k])

    KSEQ = (7, 5, 6, 3, 4, 1, 2, 0)
    products(0, at_x(2))
    for k in KSEQ:
        ra_first(k).start()
    for o in (2, 1, -1, 0):
        products(1, at_x(o))
    for m in range(4):
        rb(1, 0, m).start()
        rb(0, 0, m).start()
    products(0, at_x(1))
    for k in KSEQ:
        if k % 2 == 1:
            ra_second(k, 0).start()
    products(0, at_x(-1))
    for k in KSEQ:
        if k % 2 == 0:
            ra_second(k, 1).start()
    products(0, x)
    send_x(1)
    for m in range(4):
        step_rb(1, 1, m)
        step_rb(0, 1, m)
    for k in KSEQ:
        step_ra1(k)
    take_x(1)

    H = ND // 2

    def weigh(n, _):
        cols = pl.ds(pl.multiple_of(n * 128, 128), 128)
        ww[:, cols] = (kk[:, cols] * ub[...] * vv[:, cols]).astype(BF16)
        return 0

    def q_first(h):
        return copy(qq.at[h, 1 - c], rq.at[h], q1_send.at[h], q1_recv.at[h], other)

    def recon(h):
        part = lax.dot_general(
            ct[...], ww[h * H:(h + 1) * H, :], (((1,), (1,)), ((), ())), preferred_element_type=F32
        )
        for t in range(NL):
            qq[h, t % 2, t // 2] = part[FL * t:FL * t + FL].astype(BF16)
        q_first(h).start()

    def q_second(h, i):
        to, o = BACK[i]
        return copy(
            qq.at[h, c, at_z(o)], sq.at[h, i], q2_send.at[h, i], q2_recv.at[h, i], dev_leaf(at_z(to), c)
        )

    def step_q1(h):
        q_first(h).wait_recv()
        for o, i in ((4, 6), (3, 4), (-3, 5), (1, 0), (-1, 1), (2, None), (-2, None), (0, None)):
            add(qq.at[h, c, at_z(o)], rq[h, at_z(o)])
            if i is not None:
                q_second(h, i).start()

    def step_q2(h):
        q_second(h, 5).wait_recv()
        add(qq.at[h, c, at_z(-2)], sq[h, 5])
        q_second(h, 3).start()
        q_second(h, 4).wait_recv()
        q_second(h, 6).wait_recv()
        add(qq.at[h, c, at_z(2)], sq[h, 4], sq[h, 6])
        q_second(h, 2).start()

    def last_q(h):
        back = qq[h, c, z].astype(F32)
        for i in range(4):
            q_second(h, i).wait_recv()
            back = back + sq[h, i].astype(F32)
        cols = slice(h * H, (h + 1) * H)
        res_ref[:, cols] = (docs_ref[:, cols].astype(F32) - back).astype(BF16)

    lax.fori_loop(0, NV // 128, weigh, 0)
    recon(0)
    for m in range(4):
        step_rb(1, 2, m)
        step_rb(0, 2, m)
    recon(1)
    step_q1(0)
    step_ra2(7)
    ra_last(6).start()
    step_ra2(5)
    ra_last(5).start()
    step_ra2(6)
    ra_last(4).start()
    step_q1(1)
    for m in range(4):
        step_rb(1, 3, m)
        step_rb(0, 3, m)
    step_ra2(3)
    step_ra2(4)
    step_q2(0)
    ra_last(5).wait_recv()
    add(oa.at[x, at_y(-2)], ray[5])
    ra_last(3).start()
    ra_last(4).wait_recv()
    ra_last(6).wait_recv()
    add(oa.at[x, at_y(2)], ray[4], ray[6])
    ra_last(2).start()
    step_ra2(1)
    ra_last(1).start()
    step_ra2(2)
    ra_last(0).start()
    step_q2(1)
    for m in (3, 1, 2, 0):
        step_rb(1, 4, m)
        if m:
            rbx_copy(m).start()
    step_ra2(0)
    last_q(0)
    last_q(1)

    v = vv[...] * (1.0 / RATIO)

    def write_means(h, total):
        for g in range(2):
            at, n = COLS[2 * h + g]
            means_ref[:, at:at + n] = (total[FD * g:FD * g + FD] * v[:, at:at + n]).astype(BF16)

    took(rbx.at[pl.ds(1, 3)], rbx_recv)
    total = ob[y, x].astype(F32)
    for m in range(1, 4):
        total = total + rbx[m].astype(F32)
    write_means(1, total)
    total = oa[x, y].astype(F32)
    for i in range(4):
        ra_last(i).wait_recv()
        total = total + ray[i].astype(F32)
    write_means(0, total)

    took(dg.at[:, 0], f_send)
    for i in range(7):
        ay(i).wait_send()
        dz(i).wait_send()
        ra_last(i).wait_send()
        for h in range(2):
            q_second(h, i).wait_send()
    for s in range(4):
        for m in range(4):
            for way in range(2):
                if s < 3 or way == 1:
                    by(way, s, m, 0).wait_send()
                    rb(way, s, m).wait_send()
    for k in range(8):
        ax(k, 0).wait_send()
        ax(k, 1).wait_send()
        af(k, 0).wait_send()
        ra_first(k).wait_send()
        ra_second(k, 0).wait_send()
        ra_second(k, 1).wait_send()
    for i in range(3):
        bx(i).wait_send()
    for i in range(2):
        took(pbuf.at[i, pl.ds(0, NL - 1)], p_send.at[i])
        took(ybuf.at[i, pl.ds(0, NY - 1)], y_send.at[i])
        took(xbuf.at[i, pl.ds(0, NX - 1)], x_send.at[i])
        q_first(i).wait_send()
    took(rbx.at[pl.ds(1, 3)], rbx_send)


def body(docs, centroids):
    dma = pltpu.SemaphoreType.DMA
    residual, means = pl.pallas_call(
        kernel,
        out_shape=(jax.ShapeDtypeStruct((FL, ND), BF16), jax.ShapeDtypeStruct((FD, NV), BF16)),
        in_specs=[pl.BlockSpec(memory_space=pl.ANY)] * 2,
        out_specs=(pl.BlockSpec(memory_space=pltpu.VMEM),) * 2,
        scratch_shapes=[
            pltpu.VMEM((FL, ND), BF16),
            pltpu.VMEM((FD, NV), BF16),
            dma((2,)),
            pltpu.VMEM((NZ, 2, FL, ND), BF16),
            pltpu.VMEM((NX, NY, 2 * FD, QA), BF16),
            pltpu.VMEM((NY, NX, 2 * FD, QB), BF16),
            pltpu.VMEM((E, NV), BF16),
            pltpu.VMEM((ND, E), BF16),
            pltpu.VMEM((E, ND), BF16),
            pltpu.VMEM((ND, NV), F32),
            pltpu.VMEM((ND, NV), BF16),
            pltpu.VMEM((8, NV), F32),
            pltpu.VMEM((ND, 128), F32),
            pltpu.VMEM((ND, 128), F32),
            pltpu.VMEM((2, NL, 1, ND), F32),
            pltpu.VMEM((2, NY, 1, NV), F32),
            pltpu.VMEM((2, NX, 1, NV), F32),
            pltpu.VMEM((192, 2 * QA), F32),
            pltpu.VMEM((NX, NY, 2 * FD, QA), BF16),
            pltpu.VMEM((NY, NX, 2 * FD, QB), BF16),
            pltpu.VMEM((8, 2 * FD, QA), BF16),
            pltpu.VMEM((2, 8, 2 * FD, QA), BF16),
            pltpu.VMEM((7, 2 * FD, QA), BF16),
            pltpu.VMEM((2, 4, 4, 2 * FD, QB), BF16),
            pltpu.VMEM((4, 2 * FD, QB), BF16),
            pltpu.VMEM((2, 2, NZ, FL, ND // 2), BF16),
            pltpu.VMEM((2, NZ, FL, ND // 2), BF16),
            pltpu.VMEM((2, 7, FL, ND // 2), BF16),
            pltpu.VMEM((1, NV), F32),
            dma((7,)), dma((7,)), dma, dma,
            dma((7,)), dma((7,)), dma((8, 2)), dma((8, 2)), dma((8,)), dma((8,)),
            dma((3,)), dma((3,)), dma((2, 4, 4)), dma((2, 4, 4)),
            dma((2,)), dma((2,)), dma((2,)), dma((2,)), dma((2,)), dma((2,)),
            dma((2, 4, 4)), dma((2, 4, 4)), dma, dma,
            dma((8,)), dma((8,)), dma((2, 8)), dma((2, 8)), dma((7,)), dma((7,)),
            dma((2,)), dma((2,)), dma((2, 7)), dma((2, 7)),
        ],
        compiler_params=pltpu.CompilerParams(
            collective_id=0, has_side_effects=True, vmem_limit_bytes=48 * 2**20
        ),
        cost_estimate=pl.CostEstimate(
            flops=6 * ND * NV * E, bytes_accessed=2 * (ND * FL + NV * FD) * 2, transcendentals=ND * NV
        ),
    )(docs.T, centroids.T)
    return residual.T, means.T


def solution(mesh):
    return jax.shard_map(
        body,
        mesh=mesh,
        in_specs=(P("doc", "leaf"), P("leaf", "doc")),
        out_specs=(P("doc", "leaf"), P("leaf", "doc")),
        check_vma=False,
    )
```

time: 113 us -> 103 us (0.912); the launches traced: 112 us -> 103 us
  Pallas kernels: 108 us -> 99.7 us
    pallas_call x1, Pallas kernels: 108 us -> 99.7 us  [body(): pl.pallas_call(kernel, out_shape=(jax.ShapeDtypeStruct((FL, ND), BF16), j...]
where the time goes in v2:
time: 103 us
  Pallas kernels  99.7 us (97%)
  local copies, waits for them, and re-layouts  2.95 us (3%)
    pallas_call x1, Pallas kernels, body(): pl.pallas_call(kernel, out_shape=(jax.ShapeDtypeStruct((FL, ND), BF16), j...  99.7 us
    unnamed x6, local copies, waits for them, and re-layouts  2.95 us

profile of v2, /device:TPU:1, one launch (start us, length us, event | category | flops | bytes accessed | tf_op | source)
XLA Modules:
  0.0 103.3 jit_solution(10912680119902317543)
XLA Ops:
  0.6 0.0 copy-start
  0.6 0.9 copy-done
  1.5 0.0 copy-start.1
  1.5 0.8 copy-done.1
  2.3 99.7 %shard_map.41 = (bf16[48,512]{1,0:T(8,128)(2,1)S(1)}, bf16[24,2048]{1,0:T(8,128)(2,1)S(1)}) custom-call(bf16[48,512]{1,0:T(8,128)(2,1)S(1)} %bitcast.7, bf16[24,2048]{1,0:T(8,128)(2,1)S(1)} %bitcast.6), custom_call_target="tpu_custom_call" | custom-call | flops 4831838208 | bytes 294912 | tf_op jit(solution)/shard_map/pallas_call | solution.py:566
  102.0 0.6 copy.6
  102.6 0.6 copy.7
Async XLA Ops:
  0.6 0.9 copy-start
  1.5 0.8 copy-start.1

commit v3 on v0

v3 whole, which is shorter than its diff:
```python
import jax
import jax.numpy as jnp
from jax import lax
from jax.experimental import pallas as pl
from jax.experimental.pallas import tpu as pltpu
from jax.sharding import PartitionSpec as P

MESH = pl.DeviceIdType.MESH
F32 = jnp.float32
BF16 = jnp.bfloat16

E = 768
NX, NY, NZ, NL, NP = 4, 8, 8, 16, 4
FD, FL = 24, 48
ND, NV = 512, 2048
Q = 512
RATIO = 0.5

HOPS = ((1, 0), (-1, 0), (2, 0), (-2, 0), (1, -2), (-1, 2))
LAST_HOP = ((2, -2), (-2, 2))
BACK = ((1, 1), (-1, -1), (2, 2), (-2, -2), (1, 3), (-1, -3))
LAST_BACK = ((2, 4), (-2, -4))
ORDER = (2, 3, 0, 1)


def kernel(
    docs_ref, cent_ref, res_ref, means_ref,
    own, dg, cg, ct, xn, dt, kk, ww, ss, rr, ub, pbuf, ybuf, xbuf,
    gs, og, rc, ra1, ra2, rf, rt, qq, sq, qf, rp, vv,
    d1_send, d1_recv, d2_send, d2_recv, dz_send, dz_recv,
    cy_send, cy_recv, cw_send, cw_recv, cx_send, cx_recv, cf_send, cf_recv, cc_send, cc_recv,
    p_send, p_recv, y_send, y_recv, x_send, x_recv,
    rk_send, rk_recv, ra1_send, ra1_recv, ra2_send, ra2_recv, tf_send, tf_recv, ty_send, ty_recv,
    q_send, q_recv, qs_send, qd_send, qp_recv,
):
    d = lax.axis_index("doc")
    l = lax.axis_index("leaf")
    x, y = lax.div(d, NY), lax.rem(d, NY)
    z, a = lax.div(l, 2), lax.rem(l, 2)
    p, b = lax.div(y, 2), lax.rem(y, 2)
    odd = lax.rem(a + b, 2)
    aligned = odd == 0
    crossed = odd == 1

    def at_x(o):
        return lax.rem(x + o + NX, NX)

    def at_p(o):
        return lax.rem(p + o + 2 * NP, NP)

    def at_z(o):
        return lax.rem(z + o + NZ, NZ)

    def device(xx, yy, zz, core):
        return (xx * NY + yy, zz * 2 + core)

    to_p = (1 - odd * (1 - b), 3 - 3 * odd * b)
    from_p = (1 - odd * b, 3 - 3 * odd * (1 - b))

    def slot(n):
        if n < 2:
            return at_p(-from_p[n])
        if n == 2:
            return at_p(-from_p[0] - 1)
        return at_p(odd * (1 - from_p[1]))

    other = device(x, y, z, 1 - a)
    pair = y + 1 - 2 * b

    def copy(src, dst, s, r, to):
        return pltpu.make_async_remote_copy(
            src_ref=src, dst_ref=dst, send_sem=s, recv_sem=r, device_id=to, device_id_type=MESH
        )

    def took(ref, sem):
        pltpu.make_async_copy(ref, ref, sem).wait()

    mine_leaf = z * 2 + b
    mine_doc = p * 2 + a

    def leaf_peer(i):
        g = lax.rem(mine_leaf + i, NL)
        return device(x, 2 * p + lax.rem(g, 2), lax.div(g, 2), a)

    def doc_peer(i):
        g = lax.rem(mine_doc + i, NY)
        return device(x, 2 * lax.div(g, 2) + b, z, lax.rem(g, 2))

    def x_peer(i):
        return device(lax.rem(x + i, NX), y, z, a)

    barrier = pltpu.get_barrier_semaphore()

    def greet(to):
        pl.semaphore_signal(barrier, inc=1, device_id=to, device_id_type=MESH)

    def greet_leaf(i, _):
        greet(leaf_peer(i))
        return 0

    def greet_doc(i, _):
        greet(doc_peer(i))
        return 0

    def greet_x(i, _):
        greet(x_peer(i))
        return 0

    lax.fori_loop(1, NL, greet_leaf, 0)
    lax.fori_loop(1, NY, greet_doc, 0)
    lax.fori_loop(1, NX, greet_x, 0)

    @pl.when(crossed)
    def _():
        for w in range(2):
            greet(device(x, 2 * at_p(to_p[w]) + a, z, b))

    c32 = cent_ref[...].astype(F32)
    for h in range(2):
        at = 2 * Q * h
        own[h] = jnp.concatenate([c32[:, at:at + Q], c32[:, at + Q:at + 2 * Q]], axis=0).astype(BF16)

    @pl.when(aligned)
    def _():
        cg[a, x, p] = own[...]
        dg[z, a] = docs_ref[...]

    pl.semaphore_wait(barrier, NL - 1 + NY - 1 + NX - 1 + 2 * odd)

    def d1():
        return copy(docs_ref, dg.at[z, a], d1_send, d1_recv.at[a], device(x, pair, z, b))

    def d2():
        return copy(docs_ref, dg.at[z, a], d2_send, d2_recv, other)

    def dz(i, k):
        to, o = HOPS[i] if i < 6 else LAST_HOP[k]
        ref = dg.at[at_z(o), k]
        return copy(ref, ref, dz_send.at[i, k], dz_recv.at[i, k], device(x, y, at_z(to), a))

    def cy(w, h):
        return copy(
            own.at[h], cg.at[b, x, p, h], cy_send.at[w, h], cy_recv.at[w, h],
            device(x, 2 * at_p(to_p[w]) + a, z, b),
        )

    def cw(w, h):
        ref = cg.at[a, x, slot(w), h]
        to = 2 * at_p(1 if w == 0 else -1) + b
        return copy(ref, ref, cw_send.at[w, h], cw_recv.at[w, h], device(x, to, z, a))

    def cx(n, h, way, o=0):
        ref = cg.at[a, at_x(o), slot(n), h]
        to = at_x(1 if way == 0 else -1)
        return copy(ref, ref, cx_send.at[n, h, way], cx_recv.at[n, h, way], device(to, y, z, a))

    def cf(n, h, o):
        ref = cg.at[a, at_x(o), slot(n), h]
        to = at_x(1 if h == 0 else -1)
        return copy(ref, ref, cf_send.at[n, h], cf_recv.at[n, h], device(to, y, z, a))

    def pass_on(n, h, o):
        ref = cg.at[a, at_x(o), slot(n), h]
        copy(ref, ref, cc_send, cc_recv, other).start()

    def have(n, h):
        cx(n, h, 0).start()
        cx(n, h, 1).start()
        pass_on(n, h, 0)

    def step_y(w, h):
        cy(w, h).wait_recv()
        if w == h:
            cw(w, h).start()
        else:
            @pl.when(crossed)
            def _():
                cw(w, h).start()
        have(w, h)

    def step_w(h):
        ref = cg.at[a, x, slot(2), h]
        took(ref, cw_recv.at[(1 - odd) * h, h])
        have(2, h)

        @pl.when(crossed)
        def _():
            took(cg.at[a, x, slot(3), h], cw_recv.at[1, h])
            have(3, h)

    def step_x(n, h):
        cx(n, h, 0, -1).wait_recv()
        if h == 0:
            cf(n, h, -1).start()
        cx(n, h, 1, 1).wait_recv()
        if h == 1:
            cf(n, h, 1).start()
        pass_on(n, h, -1)
        pass_on(n, h, 1)

    def step_f(n, h):
        cf(n, h, 2).wait_recv()
        pass_on(n, h, 2)

    def step_z(i, k):
        dz(i, k).wait_recv()
        if i == 2:
            dz(4, k).start()
            if k == 0:
                dz(6, k).start()
        if i == 3:
            dz(5, k).start()
            if k == 1:
                dz(6, k).start()

    for h in range(2):
        cy(0, h).start()
        cy(1, h).start()

        @pl.when(aligned)
        def _():
            have(3, h)

        if h == 0:
            d1().start()

            @pl.when(crossed)
            def _():
                d2().start()

    @pl.when(aligned)
    def _():
        d2().wait_recv()

    @pl.when(crossed)
    def _():
        took(dg.at[z, 0], d1_recv.at[0])
        took(dg.at[z, 1], d1_recv.at[1])

    for k in range(2):
        for i in range(4):
            dz(i, k).start()

    step_y(0, 0)
    step_y(1, 0)

    @pl.when(aligned)
    def _():
        step_x(3, 0)

    step_y(0, 1)
    step_y(1, 1)

    @pl.when(aligned)
    def _():
        step_x(3, 1)
        step_f(3, 0)
        step_f(3, 1)

    step_w(0)
    for i in range(4):
        step_z(i, 0)
    step_x(0, 0)
    step_x(1, 0)
    step_w(1)
    step_x(0, 1)
    step_x(1, 1)
    for i in range(4):
        step_z(i, 1)
    step_f(0, 0)
    step_f(1, 0)
    step_x(2, 0)

    @pl.when(crossed)
    def _():
        step_x(3, 0)

    step_f(0, 1)
    step_f(1, 1)
    step_x(2, 1)

    @pl.when(crossed)
    def _():
        step_x(3, 1)

    for k in range(2):
        for i in range(4, 7):
            step_z(i, k)
    for h in range(2):
        step_f(2, h)

        @pl.when(crossed)
        def _():
            step_f(3, h)

    took(cg.at[0], cc_recv)

    dt[...] = dg[...].reshape(E, ND)
    for j in range(4):
        block = dt[:, pl.ds(128 * j, 128)].astype(F32)
        scale = 1.0 / jnp.sqrt(jnp.sum(block * block, axis=0, keepdims=True) * (1.0 / E) + 1e-06)
        xn[pl.ds(128 * j, 128), :] = (block * scale).T.astype(BF16)

    ss[...] = jnp.zeros_like(ss)

    def unpack(t, _):
        xx, pp = lax.div(t, NP), lax.rem(t, NP)
        rows = pl.ds(pl.multiple_of(t * FL, FL), FL)
        for h in range(2):
            u0, u1 = cg[0, xx, pp, h].astype(F32), cg[1, xx, pp, h].astype(F32)
            for g in range(2):
                part = jnp.concatenate([u0[FD * g:FD * g + FD], u1[FD * g:FD * g + FD]], axis=0)
                cols = pl.ds((2 * h + g) * Q, Q)
                ct[rows, cols] = part.astype(BF16)
                ss[:, cols] += jnp.sum((part * part).reshape(FL // 8, 8, Q), axis=0)
        return 0

    lax.fori_loop(0, NX * NP, unpack, 0)

    rr[...] = jnp.zeros_like(rr)
    T = 256

    def scores(n, _):
        cols = pl.ds(pl.multiple_of(n * T, T), T)
        norm = jnp.sqrt(jnp.sum(ss[:, cols], axis=0, keepdims=True) * (1.0 / E) + 1e-06)
        s = jnp.dot(xn[...], ct[:, cols], preferred_element_type=F32)
        k = jnp.exp(s * (1.0 / (E * 0.02 * norm)))
        kk[:, cols] = k
        rr[...] += k[:, 0:128] + k[:, 128:256]
        return 0

    lax.fori_loop(0, NV // T, scores, 0)

    def reduce_leaf(i):
        pbuf[i, mine_leaf] = jnp.sum(rr[...].T, axis=0, keepdims=True)

        def send(j, _):
            ref = pbuf.at[i, mine_leaf]
            copy(ref, ref, p_send.at[i], p_recv.at[i], leaf_peer(j)).start()
            return 0

        lax.fori_loop(1, NL, send, 0)
        took(pbuf.at[i, pl.ds(0, NL - 1)], p_recv.at[i])
        u = 1.0 / jnp.sum(pbuf[i], axis=0)
        ub[...] = jnp.broadcast_to(u, (128, ND)).T

    def columns(i):
        def one(n, _):
            cols = pl.ds(pl.multiple_of(n * 128, 128), 128)
            w = kk[:, cols] * ub[...]
            if i == 1:
                ww[:, cols] = w.astype(BF16)
            total = jnp.sum(jnp.sum(w.reshape(ND // 8, 8, 128), axis=0), axis=0, keepdims=True)
            ybuf[i, mine_doc, :, cols] = total
            return 0

        lax.fori_loop(0, NV // 128, one, 0)

    def send_y(i):
        def send(j, _):
            ref = ybuf.at[i, mine_doc]
            copy(ref, ref, y_send.at[i], y_recv.at[i], doc_peer(j)).start()
            return 0

        lax.fori_loop(1, NY, send, 0)

    def send_x(i):
        took(ybuf.at[i, pl.ds(0, NY - 1)], y_recv.at[i])
        xbuf[i, x] = jnp.sum(ybuf[i], axis=0)

        def send(j, _):
            copy(xbuf.at[i, x], xbuf.at[i, x], x_send.at[i], x_recv.at[i], x_peer(j)).start()
            return 0

        lax.fori_loop(1, NX, send, 0)

    def take_x(i):
        took(xbuf.at[i, pl.ds(0, NX - 1)], x_recv.at[i])
        vv[...] = RATIO / jnp.sum(xbuf[i], axis=0)

    reduce_leaf(0)
    columns(0)
    send_y(0)
    send_x(0)
    take_x(0)

    rr[...] = jnp.zeros_like(rr)

    def rows_of(n, _):
        cols = pl.ds(pl.multiple_of(n * 128, 128), 128)
        rr[...] += kk[:, cols] * vv[:, cols]
        return 0

    lax.fori_loop(0, NV // 128, rows_of, 0)
    reduce_leaf(1)
    columns(1)
    send_y(1)

    XSEQ = (2, 1, -1, 0)

    def products(i):
        xx = at_x(XSEQ[i])
        rows = pl.ds(pl.multiple_of(xx * 192, 192), 192)
        gs[...] = jnp.dot(dt[rows, :], ww[...], preferred_element_type=F32)
        for yy in range(NY):
            r = FD * yy
            for h in range(2):
                at = 2 * Q * h
                unit = jnp.concatenate([gs[r:r + FD, at:at + Q], gs[r:r + FD, at + Q:at + 2 * Q]], axis=0)
                og[yy % 2, xx, yy // 2, h] = unit.astype(BF16)
        across(i).start()

    def across(i):
        xx = at_x(XSEQ[i])
        return copy(og.at[1 - a, xx], rc.at[xx], rk_send.at[i], rk_recv.at[i], other)

    def add(o, n, h, *others):
        ref = og.at[a, at_x(o), slot(n), h]
        total = ref[...].astype(F32) + rc[at_x(o), slot(n), h].astype(F32)
        for one in others:
            total = total + one.astype(F32)
        return ref, total

    def ra_first(n, h):
        to = at_x(1 if h == 0 else -1)
        return copy(
            og.at[a, at_x(2), slot(n), h], ra1.at[n, h], ra1_send.at[n, h], ra1_recv.at[n, h],
            device(to, y, z, a),
        )

    def ra_second(n, h, way):
        to = at_x(1 if way == 0 else -1)
        return copy(
            og.at[a, to, slot(n), h], ra2.at[way, n, h], ra2_send.at[way, n, h], ra2_recv.at[way, n, h],
            device(to, y, z, a),
        )

    def tf(w, n, h):
        to = 2 * at_p(2 * w - 1) + b
        return copy(og.at[a, x, slot(n), h], rf.at[w, h], tf_send.at[n - 2, h], tf_recv.at[w, h], device(x, to, z, a))

    def ty(n, h):
        return copy(
            og.at[a, x, slot(n), h], rt.at[n, h], ty_send.at[n, h], ty_recv.at[n, h],
            device(x, 2 * slot(n) + a, z, b),
        )

    def step_first():
        for n in ORDER:
            for h in range(2):
                ref, total = add(2, n, h)
                ref[...] = total.astype(BF16)
                ra_first(n, h).start()

    def step_plain(way):
        h = 1 - way
        for n in ORDER:
            ref, total = add(1 if way == 0 else -1, n, h)
            ref[...] = total.astype(BF16)
            ra_second(n, h, way).start()

    def step_joined(n, h):
        ra_first(n, h).wait_recv()
        ref, total = add(1 if h == 0 else -1, n, h, ra1[n, h])
        ref[...] = total.astype(BF16)
        ra_second(n, h, h).start()

    def step_home(n, h):
        ra_second(n, h, 0).wait_recv()
        ra_second(n, h, 1).wait_recv()
        ref, total = add(0, n, h, ra2[0, n, h], ra2[1, n, h])
        at = 2 * Q * h
        low = total[0:FD] * (vv[:, at:at + Q] * (1.0 / RATIO))
        high = total[FD:2 * FD] * (vv[:, at + Q:at + 2 * Q] * (1.0 / RATIO))
        total = jnp.concatenate([low, high], axis=0)
        if n < 2:
            if n == h:
                tf(n, 2, h).wait_recv()
            else:
                @pl.when(crossed)
                def _():
                    tf(n, 2, h).wait_recv()
            total = total + rf[n, h].astype(F32)
        ref[...] = total.astype(BF16)
        if n < 2:
            ty(n, h).start()
        if n == 2:
            tf((1 - odd) * h, n, h).start()
        if n == 3:
            @pl.when(crossed)
            def _():
                tf(1, n, h).start()

            @pl.when(aligned)
            def _():
                rt[2, h] = ref[...]

    @pl.when(aligned)
    def _():
        rf[0, 1] = jnp.zeros((2 * FD, Q), BF16)
        rf[1, 0] = jnp.zeros((2 * FD, Q), BF16)

    @pl.when(crossed)
    def _():
        rt[2] = jnp.zeros((2, 2 * FD, Q), BF16)

    H = ND // 2

    def weigh(n, _):
        cols = pl.ds(pl.multiple_of(n * 128, 128), 128)
        ww[:, cols] = (kk[:, cols] * ub[...] * vv[:, cols]).astype(BF16)
        return 0

    def qz(h, i):
        to, o = BACK[i] if i < 6 else LAST_BACK[h]
        return copy(
            qq.at[h, at_z(o)], sq.at[h, i], q_send.at[h, i], q_recv.at[h, i], device(x, y, at_z(to), a)
        )

    def recon(h):
        part = lax.dot_general(
            ct[...], ww[h * H:(h + 1) * H, :], (((1,), (1,)), ((), ())), preferred_element_type=F32
        )
        for t in range(NL):
            qq[h, t // 2, t % 2] = part[FL * t:FL * t + FL].astype(BF16)
        for i in (6, 4, 5, 0, 1):
            qz(h, i).start()

    def step_q(h):
        for w, (o, into, out) in enumerate(((2, 4, 2), (-2, 5, 3))):
            ref = qq.at[h, at_z(o)]
            qz(h, into).wait_recv()
            total = ref[...].astype(F32) + sq[h, into].astype(F32)
            if w == h:
                qz(h, 6).wait_recv()
                total = total + sq[h, 6].astype(F32)
            ref[...] = total.astype(BF16)
            qz(h, out).start()

    def q_same(h):
        return copy(qf.at[h, a], rp.at[h, 1], qs_send.at[h], qp_recv.at[h, 1], device(x, 2 * p + a, z, a))

    def q_diff(h):
        return copy(
            qf.at[h, 1 - a], rp.at[h, odd], qd_send.at[h], qp_recv.at[h, odd], device(x, 2 * p + a, z, 1 - a)
        )

    def step_pair(h):
        total = qq[h, z].astype(F32)
        for i in range(4):
            qz(h, i).wait_recv()
            total = total + sq[h, i].astype(F32)
        qf[h] = total.astype(BF16)

        @pl.when(crossed)
        def _():
            q_same(h).start()

        @pl.when(aligned)
        def _():
            rp[h, 0] = qf[h, a]

        q_diff(h).start()

    def last_q(h):
        took(rp.at[h, 1], qp_recv.at[h, 1])

        @pl.when(crossed)
        def _():
            took(rp.at[h, 0], qp_recv.at[h, 0])

        cols = slice(h * H, (h + 1) * H)
        back = rp[h, 0].astype(F32) + rp[h, 1].astype(F32)
        res_ref[:, cols] = (docs_ref[:, cols].astype(F32) - back).astype(BF16)

    products(0)
    products(1)
    across(0).wait_recv()
    step_first()
    products(2)
    across(1).wait_recv()
    step_plain(0)
    products(3)
    across(2).wait_recv()
    step_plain(1)
    send_x(1)
    for n in ORDER:
        step_joined(n, 0)
        step_joined(n, 1)
    across(3).wait_recv()
    for i in range(4):
        across(i).wait_send()
    take_x(1)
    lax.fori_loop(0, NV // 128, weigh, 0)
    recon(0)
    for h in range(2):
        step_home(2, h)
    recon(1)
    for h in range(2):
        step_home(3, h)
    step_q(0)
    for h in range(2):
        step_home(0, h)
        step_home(1, h)
    step_q(1)
    step_pair(0)
    step_pair(1)

    for h in range(2):
        total = rt[2, h].astype(F32)
        for n in range(2):
            ty(n, h).wait_recv()
            total = total + rt[n, h].astype(F32)
        at = 2 * Q * h
        means_ref[:, at:at + Q] = total[0:FD].astype(BF16)
        means_ref[:, at + Q:at + 2 * Q] = total[FD:2 * FD].astype(BF16)

    last_q(0)
    last_q(1)

    d1().wait_send()

    @pl.when(crossed)
    def _():
        d2().wait_send()
        cw(0, 1).wait_send()
        cw(1, 0).wait_send()
        for h in range(2):
            tf(1, 3, h).wait_send()
            q_same(h).wait_send()

    for h in range(2):
        cw(h, h).wait_send()
        tf(0, 2, h).wait_send()
        q_diff(h).wait_send()
        for i in range(7):
            qz(h, i).wait_send()
            dz(i, h).wait_send()
        for n in range(4):
            if n < 2:
                cy(n, h).wait_send()
                ty(n, h).wait_send()
            cf(n, h, 0).wait_send()
            ra_first(n, h).wait_send()
            for way in range(2):
                cx(n, h, way).wait_send()
                ra_second(n, h, way).wait_send()
    took(cg.at[0], cc_send)
    for i in range(2):
        took(pbuf.at[i, pl.ds(0, NL - 1)], p_send.at[i])
        took(ybuf.at[i, pl.ds(0, NY - 1)], y_send.at[i])
        took(xbuf.at[i, pl.ds(0, NX - 1)], x_send.at[i])


def body(docs, centroids):
    dma = pltpu.SemaphoreType.DMA
    unit = (2 * FD, Q)
    residual, means = pl.pallas_call(
        kernel,
        out_shape=(jax.ShapeDtypeStruct((FL, ND), BF16), jax.ShapeDtypeStruct((FD, NV), BF16)),
        in_specs=[pl.BlockSpec(memory_space=pltpu.VMEM)] * 2,
        out_specs=(pl.BlockSpec(memory_space=pltpu.VMEM),) * 2,
        scratch_shapes=[
            pltpu.VMEM((2, *unit), BF16),
            pltpu.VMEM((NZ, 2, FL, ND), BF16),
            pltpu.VMEM((2, NX, NP, 2, *unit), BF16),
            pltpu.VMEM((E, NV), BF16),
            pltpu.VMEM((ND, E), BF16),
            pltpu.VMEM((E, ND), BF16),
            pltpu.VMEM((ND, NV), F32),
            pltpu.VMEM((ND, NV), BF16),
            pltpu.VMEM((8, NV), F32),
            pltpu.VMEM((ND, 128), F32),
            pltpu.VMEM((ND, 128), F32),
            pltpu.VMEM((2, NL, 1, ND), F32),
            pltpu.VMEM((2, NY, 1, NV), F32),
            pltpu.VMEM((2, NX, 1, NV), F32),
            pltpu.VMEM((192, NV), F32),
            pltpu.VMEM((2, NX, NP, 2, *unit), BF16),
            pltpu.VMEM((NX, NP, 2, *unit), BF16),
            pltpu.VMEM((NP, 2, *unit), BF16),
            pltpu.VMEM((2, NP, 2, *unit), BF16),
            pltpu.VMEM((2, 2, *unit), BF16),
            pltpu.VMEM((3, 2, *unit), BF16),
            pltpu.VMEM((2, NZ, 2, FL, ND // 2), BF16),
            pltpu.VMEM((2, 7, 2, FL, ND // 2), BF16),
            pltpu.VMEM((2, 2, FL, ND // 2), BF16),
            pltpu.VMEM((2, 2, FL, ND // 2), BF16),
            pltpu.VMEM((1, NV), F32),
            dma, dma((2,)), dma, dma, dma((7, 2)), dma((7, 2)),
            dma((2, 2)), dma((2, 2)), dma((2, 2)), dma((2, 2)), dma((NP, 2, 2)), dma((NP, 2, 2)), dma((NP, 2)), dma((NP, 2)), dma, dma,
            dma((2,)), dma((2,)), dma((2,)), dma((2,)), dma((2,)), dma((2,)),
            dma((4,)), dma((4,)), dma((NP, 2)), dma((NP, 2)), dma((2, NP, 2)), dma((2, NP, 2)),
            dma((2, 2)), dma((2, 2)), dma((2, 2)), dma((2, 2)),
            dma((2, 7)), dma((2, 7)), dma((2,)), dma((2,)), dma((2, 2)),
        ],
        compiler_params=pltpu.CompilerParams(
            collective_id=0, has_side_effects=True, vmem_limit_bytes=48 * 2**20
        ),
        cost_estimate=pl.CostEstimate(
            flops=6 * ND * NV * E, bytes_accessed=2 * (ND * FL + NV * FD) * 2, transcendentals=ND * NV
        ),
    )(docs.T, centroids.T)
    return residual.T, means.T


def solution(mesh):
    return jax.shard_map(
        body,
        mesh=mesh,
        in_specs=(P("doc", "leaf"), P("leaf", "doc")),
        out_specs=(P("doc", "leaf"), P("leaf", "doc")),
        check_vma=False,
    )
```

time: 614 us -> 103 us (0.17)
  waiting for transfers between devices: 347 us -> 0 us
  blocking collectives: 209 us -> 0 us
  Pallas kernels: 0 us -> 99.3 us
  matrix products: 32.9 us -> 0 us
  between operations: 13.8 us -> 0.65 us
    reduce_scatter x2 -> x0, waiting for transfers between devices: 283 us -> none  [the longest x1 223 us: body(): lax.psum_scatter(sums_part.astype(jnp.bfloat16), 'doc', scatter_dimension...]
    psum x4 -> x0, blocking collectives: 182 us -> none  [the longest x2 117 us: body(): scales_v = ratio / lax.psum(column_portion, 'doc')]
    pallas_call x0 -> x1, Pallas kernels: none -> 99.3 us  [body(): pl.pallas_call(kernel, out_shape=(jax.ShapeDtypeStruct((FL, ND), BF16), j...]
    all_gather x1 -> x0, waiting for transfers between devices: 63.2 us -> none  [body(): leaf_row_block = lax.all_gather(centroids, 'doc', axis=1, tiled=True)]
    dot_general x7 -> x0, matrix products: 32.9 us -> none  [the longest x2 9.53 us: body(): row_portion = jnp.dot(kernel, scales_v, precision=lax.Precision.HIGHEST)]
    all_gather x1 -> x0, blocking collectives: 26.9 us -> none  [body(): document_row_block = lax.all_gather(docs, 'leaf', axis=1, tiled=True)]
  transfers between devices with their start and end apart: 3 -> 0, of which waited for: 3 -> 0; matrix products, arithmetic and copies ran while one was open for 1% -> 0% of each run, Pallas kernels for 0% -> 0%
where the time goes in v3:
time: 103 us
  Pallas kernels  99.3 us (96%)
  local copies, waits for them, and re-layouts  2.95 us (3%)
    pallas_call x1, Pallas kernels, body(): pl.pallas_call(kernel, out_shape=(jax.ShapeDtypeStruct((FL, ND), BF16), j...  99.3 us
    unnamed x6, local copies, waits for them, and re-layouts  2.95 us

profile of v3, /device:TPU:1, one launch (start us, length us, event | category | flops | bytes accessed | tf_op | source)
XLA Modules:
  0.0 102.9 jit_solution(16963222511622757056)
XLA Ops:
  0.6 0.0 copy-start
  0.6 0.9 copy-done
  1.5 0.0 copy-start.1
  1.5 0.8 copy-done.1
  2.3 99.3 %shard_map.41 = (bf16[48,512]{1,0:T(8,128)(2,1)S(1)}, bf16[24,2048]{1,0:T(8,128)(2,1)S(1)}) custom-call(bf16[48,512]{1,0:T(8,128)(2,1)S(1)} %bitcast.7, bf16[24,2048]{1,0:T(8,128)(2,1)S(1)} %bitcast.6), custom_call_target="tpu_custom_call" | custom-call | flops 4831838208 | bytes 294912 | tf_op jit(solution)/shard_map/pallas_call | solution.py:658
  101.7 0.6 copy.6
  102.3 0.6 copy.7
Async XLA Ops:
  0.6 0.9 copy-start
  1.5 0.8 copy-start.1

commit v4 on v3

--- a/solution.py
+++ b/solution.py
@@ -14,24 +14,27 @@
 FD, FL = 24, 48
 ND, NV = 512, 2048
 Q = 512
+QA, QB = 384, 256
+LATE = 4 * QA
 RATIO = 0.5
 
 HOPS = ((1, 0), (-1, 0), (2, 0), (-2, 0), (1, -2), (-1, 2))
 LAST_HOP = ((2, -2), (-2, 2))
-BACK = ((1, 1), (-1, -1), (2, 2), (-2, -2), (1, 3), (-1, -3))
+BACK = ((1, 3), (-1, -3))
 LAST_BACK = ((2, 4), (-2, -4))
 ORDER = (2, 3, 0, 1)
 
 
 def kernel(
     docs_ref, cent_ref, res_ref, means_ref,
-    own, dg, cg, ct, xn, dt, kk, ww, ss, rr, ub, pbuf, ybuf, xbuf,
-    gs, og, rc, ra1, ra2, rf, rt, qq, sq, qf, rp, vv,
+    own, gb, dg, cg, cgb, ct, xn, dt, kk, ww, ss, rr, ub, pbuf, ybuf, xbuf,
+    gs, og, rc, ra1, ra2, rf, rt, qq, sq, rp, vv,
     d1_send, d1_recv, d2_send, d2_recv, dz_send, dz_recv,
+    bx_send, bx_recv, by_send, by_recv, bw_send, bw_recv, bc_send, bc_recv,
     cy_send, cy_recv, cw_send, cw_recv, cx_send, cx_recv, cf_send, cf_recv, cc_send, cc_recv,
     p_send, p_recv, y_send, y_recv, x_send, x_recv,
     rk_send, rk_recv, ra1_send, ra1_recv, ra2_send, ra2_recv, tf_send, tf_recv, ty_send, ty_recv,
-    q_send, q_recv, qs_send, qd_send, qp_recv,
+    q_send, q_recv, qh_send, qh_recv,
 ):
     d = lax.axis_index("doc")
     l = lax.axis_index("leaf")
@@ -114,18 +117,24 @@
     def _():
         for w in range(2):
             greet(device(x, 2 * at_p(to_p[w]) + a, z, b))
+        for o in (1, -1, 2, -2):
+            greet(device(x, pair, at_z(o), 1 - a))
+
+    for o in (1, -1, 2, -2):
+        greet(device(x, y, at_z(o), 1 - a))
 
     c32 = cent_ref[...].astype(F32)
     for h in range(2):
-        at = 2 * Q * h
-        own[h] = jnp.concatenate([c32[:, at:at + Q], c32[:, at + Q:at + 2 * Q]], axis=0).astype(BF16)
+        at = 2 * QA * h
+        own[h] = jnp.concatenate([c32[:, at:at + QA], c32[:, at + QA:at + 2 * QA]], axis=0).astype(BF16)
+    gb[x] = jnp.concatenate([c32[:, LATE:LATE + QB], c32[:, LATE + QB:]], axis=0).astype(BF16)
 
     @pl.when(aligned)
     def _():
         cg[a, x, p] = own[...]
         dg[z, a] = docs_ref[...]
 
-    pl.semaphore_wait(barrier, NL - 1 + NY - 1 + NX - 1 + 2 * odd)
+    pl.semaphore_wait(barrier, NL - 1 + NY - 1 + NX - 1 + 4 + 6 * odd)
 
     def d1():
         return copy(docs_ref, dg.at[z, a], d1_send, d1_recv.at[a], device(x, pair, z, b))
@@ -156,16 +165,71 @@
 
     def cf(n, h, o):
         ref = cg.at[a, at_x(o), slot(n), h]
-        to = at_x(1 if h == 0 else -1)
+        to = at_x(2 if n >= 2 else 1 if h == 0 else -1)
         return copy(ref, ref, cf_send.at[n, h], cf_recv.at[n, h], device(to, y, z, a))
 
     def pass_on(n, h, o):
         ref = cg.at[a, at_x(o), slot(n), h]
         copy(ref, ref, cc_send, cc_recv, other).start()
 
+    def bx(i):
+        to = at_x((1, -1, 2)[i])
+        return copy(gb.at[x], gb.at[x], bx_send.at[i], bx_recv.at[i], device(to, y, z, a))
+
+    def by(w, h):
+        half = pl.ds(2 * h, 2)
+        return copy(
+            gb.at[half], cgb.at[b, p, half], by_send.at[w, h], by_recv.at[w, h],
+            device(x, 2 * at_p(to_p[w]) + a, z, b),
+        )
+
+    def bw(w, h):
+        ref = cgb.at[a, slot(w), pl.ds(2 * h, 2)]
+        to = 2 * at_p(1 if w == 0 else -1) + b
+        return copy(ref, ref, bw_send.at[w, h], bw_recv.at[w, h], device(x, to, z, a))
+
+    def pass_b(n, h):
+        ref = cgb.at[a, slot(n), pl.ds(2 * h, 2)]
+        copy(ref, ref, bc_send, bc_recv, other).start()
+
+    def step_bx():
+        for i in range(3):
+            bx(i).wait_recv()
+        for h in range(2):
+            by(0, h).start()
+            by(1, h).start()
+
+        @pl.when(aligned)
+        def _():
+            cgb[a, p] = gb[...]
+            pass_b(3, 0)
+            pass_b(3, 1)
+
+    def step_by(w, h):
+        by(w, h).wait_recv()
+        if w == h:
+            bw(w, h).start()
+        else:
+            @pl.when(crossed)
+            def _():
+                bw(w, h).start()
+        pass_b(w, h)
+
+    def step_bw(h):
+        half = pl.ds(2 * h, 2)
+        took(cgb.at[a, slot(2), half], bw_recv.at[(1 - odd) * h, h])
+        pass_b(2, h)
+
+        @pl.when(crossed)
+        def _():
+            took(cgb.at[a, slot(3), half], bw_recv.at[1, h])
+            pass_b(3, h)
+
     def have(n, h):
         cx(n, h, 0).start()
         cx(n, h, 1).start()
+        if n >= 2:
+            cf(n, h, 0).start()
         pass_on(n, h, 0)
 
     def step_y(w, h):
@@ -190,10 +254,10 @@
 
     def step_x(n, h):
         cx(n, h, 0, -1).wait_recv()
-        if h == 0:
+        if h == 0 and n < 2:
             cf(n, h, -1).start()
         cx(n, h, 1, 1).wait_recv()
-        if h == 1:
+        if h == 1 and n < 2:
             cf(n, h, 1).start()
         pass_on(n, h, -1)
         pass_on(n, h, 1)
@@ -216,6 +280,9 @@
     for h in range(2):
         cy(0, h).start()
         cy(1, h).start()
+        if h == 0:
+            for i in range(3):
+                bx(i).start()
 
         @pl.when(aligned)
         def _():
@@ -250,6 +317,7 @@
 
     step_y(0, 1)
     step_y(1, 1)
+    step_bx()
 
     @pl.when(aligned)
     def _():
@@ -263,6 +331,9 @@
     step_x(0, 0)
     step_x(1, 0)
     step_w(1)
+    for h in range(2):
+        step_by(0, h)
+        step_by(1, h)
     step_x(0, 1)
     step_x(1, 1)
     for i in range(4):
@@ -275,6 +346,7 @@
     def _():
         step_x(3, 0)
 
+    step_bw(0)
     step_f(0, 1)
     step_f(1, 1)
     step_x(2, 1)
@@ -293,7 +365,9 @@
         def _():
             step_f(3, h)
 
+    step_bw(1)
     took(cg.at[0], cc_recv)
+    took(cgb.at[0], bc_recv)
 
     dt[...] = dg[...].reshape(E, ND)
     for j in range(4):
@@ -306,13 +380,16 @@
     def unpack(t, _):
         xx, pp = lax.div(t, NP), lax.rem(t, NP)
         rows = pl.ds(pl.multiple_of(t * FL, FL), FL)
-        for h in range(2):
-            u0, u1 = cg[0, xx, pp, h].astype(F32), cg[1, xx, pp, h].astype(F32)
+        for h in range(3):
+            if h < 2:
+                u0, u1, n = cg[0, xx, pp, h].astype(F32), cg[1, xx, pp, h].astype(F32), QA
+            else:
+                u0, u1, n = cgb[0, pp, xx].astype(F32), cgb[1, pp, xx].astype(F32), QB
             for g in range(2):
                 part = jnp.concatenate([u0[FD * g:FD * g + FD], u1[FD * g:FD * g + FD]], axis=0)
-                cols = pl.ds((2 * h + g) * Q, Q)
+                cols = pl.ds(2 * QA * h + n * g, n)
                 ct[rows, cols] = part.astype(BF16)
-                ss[:, cols] += jnp.sum((part * part).reshape(FL // 8, 8, Q), axis=0)
+                ss[:, cols] += jnp.sum((part * part).reshape(FL // 8, 8, n), axis=0)
         return 0
 
     lax.fori_loop(0, NX * NP, unpack, 0)
@@ -351,12 +428,22 @@
             if i == 1:
                 ww[:, cols] = w.astype(BF16)
             total = jnp.sum(jnp.sum(w.reshape(ND // 8, 8, 128), axis=0), axis=0, keepdims=True)
-            ybuf[i, mine_doc, :, cols] = total
+            xbuf[i, x, :, cols] = total
             return 0
 
         lax.fori_loop(0, NV // 128, one, 0)
 
+    def send_x(i):
+        def send(j, _):
+            copy(xbuf.at[i, x], xbuf.at[i, x], x_send.at[i], x_recv.at[i], x_peer(j)).start()
+            return 0
+
+        lax.fori_loop(1, NX, send, 0)
+
     def send_y(i):
+        took(xbuf.at[i, pl.ds(0, NX - 1)], x_recv.at[i])
+        ybuf[i, mine_doc] = jnp.sum(xbuf[i], axis=0)
+
         def send(j, _):
             ref = ybuf.at[i, mine_doc]
             copy(ref, ref, y_send.at[i], y_recv.at[i], doc_peer(j)).start()
@@ -364,25 +451,15 @@
 
         lax.fori_loop(1, NY, send, 0)
 
-    def send_x(i):
+    def take_y(i):
         took(ybuf.at[i, pl.ds(0, NY - 1)], y_recv.at[i])
-        xbuf[i, x] = jnp.sum(ybuf[i], axis=0)
-
-        def send(j, _):
-            copy(xbuf.at[i, x], xbuf.at[i, x], x_send.at[i], x_recv.at[i], x_peer(j)).start()
-            return 0
-
-        lax.fori_loop(1, NX, send, 0)
-
-    def take_x(i):
-        took(xbuf.at[i, pl.ds(0, NX - 1)], x_recv.at[i])
-        vv[...] = RATIO / jnp.sum(xbuf[i], axis=0)
+        vv[...] = RATIO / jnp.sum(ybuf[i], axis=0)
 
     reduce_leaf(0)
     columns(0)
+    send_x(0)
     send_y(0)
-    send_x(0)
-    take_x(0)
+    take_y(0)
 
     rr[...] = jnp.zeros_like(rr)
 
@@ -394,7 +471,7 @@
     lax.fori_loop(0, NV // 128, rows_of, 0)
     reduce_leaf(1)
     columns(1)
-    send_y(1)
+    send_x(1)
 
     XSEQ = (2, 1, -1, 0)
 
@@ -453,11 +530,12 @@
                 ra_first(n, h).start()
 
     def step_plain(way):
-        h = 1 - way
         for n in ORDER:
-            ref, total = add(1 if way == 0 else -1, n, h)
-            ref[...] = total.astype(BF16)
-            ra_second(n, h, way).start()
+            for h in range(2):
+                if h != way:
+                    ref, total = add(1 if way == 0 else -1, n, h)
+                    ref[...] = total.astype(BF16)
+                    ra_second(n, h, way).start()
 
     def step_joined(n, h):
         ra_first(n, h).wait_recv()
@@ -512,10 +590,27 @@
         return 0
 
     def qz(h, i):
-        to, o = BACK[i] if i < 6 else LAST_BACK[h]
+        to, o = BACK[i] if i < 2 else LAST_BACK[h]
         return copy(
             qq.at[h, at_z(o)], sq.at[h, i], q_send.at[h, i], q_recv.at[h, i], device(x, y, at_z(to), a)
         )
+
+    def q_home(h, o, e):
+        to = device(x, 2 * p + a, at_z(o), e)
+        copy(qq.at[h, at_z(o), e], rp.at[h, 2 * (o + 2) + b], qh_send.at[h], qh_recv.at[h], to).start()
+
+    def send_home(h, o):
+        q_home(h, o, 1 - a)
+        if o:
+            q_home(h, o, a)
+        else:
+            @pl.when(crossed)
+            def _():
+                q_home(h, o, a)
+
+            @pl.when(aligned)
+            def _():
+                rp[h, 2 * (o + 2) + b] = qq[h, z, a]
 
     def recon(h):
         part = lax.dot_general(
@@ -523,54 +618,37 @@
         )
         for t in range(NL):
             qq[h, t // 2, t % 2] = part[FL * t:FL * t + FL].astype(BF16)
-        for i in (6, 4, 5, 0, 1):
+        for i in (2, 0, 1):
             qz(h, i).start()
+        for o in (1, -1, 0):
+            send_home(h, o)
 
     def step_q(h):
-        for w, (o, into, out) in enumerate(((2, 4, 2), (-2, 5, 3))):
+        for w, o in enumerate((2, -2)):
             ref = qq.at[h, at_z(o)]
-            qz(h, into).wait_recv()
-            total = ref[...].astype(F32) + sq[h, into].astype(F32)
+            qz(h, w).wait_recv()
+            total = ref[...].astype(F32) + sq[h, w].astype(F32)
             if w == h:
-                qz(h, 6).wait_recv()
-                total = total + sq[h, 6].astype(F32)
+                qz(h, 2).wait_recv()
+                total = total + sq[h, 2].astype(F32)
             ref[...] = total.astype(BF16)
-            qz(h, out).start()
-
-    def q_same(h):
-        return copy(qf.at[h, a], rp.at[h, 1], qs_send.at[h], qp_recv.at[h, 1], device(x, 2 * p + a, z, a))
-
-    def q_diff(h):
-        return copy(
-            qf.at[h, 1 - a], rp.at[h, odd], qd_send.at[h], qp_recv.at[h, odd], device(x, 2 * p + a, z, 1 - a)
-        )
-
-    def step_pair(h):
-        total = qq[h, z].astype(F32)
-        for i in range(4):
-            qz(h, i).wait_recv()
-            total = total + sq[h, i].astype(F32)
-        qf[h] = total.astype(BF16)
-
+            send_home(h, o)
+
+    def wait_home(h, sem):
         @pl.when(crossed)
         def _():
-            q_same(h).start()
+            took(rp.at[h], sem.at[h])
 
         @pl.when(aligned)
         def _():
-            rp[h, 0] = qf[h, a]
-
-        q_diff(h).start()
+            took(rp.at[h, pl.ds(0, 9)], sem.at[h])
 
     def last_q(h):
-        took(rp.at[h, 1], qp_recv.at[h, 1])
-
-        @pl.when(crossed)
-        def _():
-            took(rp.at[h, 0], qp_recv.at[h, 0])
-
+        wait_home(h, qh_recv)
         cols = slice(h * H, (h + 1) * H)
-        back = rp[h, 0].astype(F32) + rp[h, 1].astype(F32)
+        back = rp[h, 0].astype(F32)
+        for i in range(1, 10):
+            back = back + rp[h, i].astype(F32)
         res_ref[:, cols] = (docs_ref[:, cols].astype(F32) - back).astype(BF16)
 
     products(0)
@@ -578,19 +656,19 @@
     across(0).wait_recv()
     step_first()
     products(2)
+    send_y(1)
     across(1).wait_recv()
     step_plain(0)
     products(3)
     across(2).wait_recv()
     step_plain(1)
-    send_x(1)
     for n in ORDER:
         step_joined(n, 0)
         step_joined(n, 1)
     across(3).wait_recv()
     for i in range(4):
         across(i).wait_send()
-    take_x(1)
+    take_y(1)
     lax.fori_loop(0, NV // 128, weigh, 0)
     recon(0)
     for h in range(2):
@@ -599,12 +677,11 @@
     for h in range(2):
         step_home(3, h)
     step_q(0)
-    for h in range(2):
-        step_home(0, h)
-        step_home(1, h)
+    step_home(0, 0)
+    step_home(1, 0)
     step_q(1)
-    step_pair(0)
-    step_pair(1)
+    step_home(0, 1)
+    step_home(1, 1)
 
     for h in range(2):
         total = rt[2, h].astype(F32)
@@ -625,27 +702,34 @@
         d2().wait_send()
         cw(0, 1).wait_send()
         cw(1, 0).wait_send()
+        bw(0, 1).wait_send()
+        bw(1, 0).wait_send()
         for h in range(2):
             tf(1, 3, h).wait_send()
-            q_same(h).wait_send()
 
     for h in range(2):
         cw(h, h).wait_send()
+        bw(h, h).wait_send()
         tf(0, 2, h).wait_send()
-        q_diff(h).wait_send()
+        wait_home(h, qh_send)
         for i in range(7):
-            qz(h, i).wait_send()
+            if i < 3:
+                qz(h, i).wait_send()
             dz(i, h).wait_send()
         for n in range(4):
             if n < 2:
                 cy(n, h).wait_send()
+                by(n, h).wait_send()
                 ty(n, h).wait_send()
             cf(n, h, 0).wait_send()
             ra_first(n, h).wait_send()
             for way in range(2):
                 cx(n, h, way).wait_send()
                 ra_second(n, h, way).wait_send()
+    for i in range(3):
+        bx(i).wait_send()
     took(cg.at[0], cc_send)
+    took(cgb.at[0], bc_send)
     for i in range(2):
         took(pbuf.at[i, pl.ds(0, NL - 1)], p_send.at[i])
         took(ybuf.at[i, pl.ds(0, NY - 1)], y_send.at[i])
@@ -661,9 +745,11 @@
         in_specs=[pl.BlockSpec(memory_space=pltpu.VMEM)] * 2,
         out_specs=(pl.BlockSpec(memory_space=pltpu.VMEM),) * 2,
         scratch_shapes=[
-            pltpu.VMEM((2, *unit), BF16),
+            pltpu.VMEM((2, 2 * FD, QA), BF16),
+            pltpu.VMEM((NX, 2 * FD, QB), BF16),
             pltpu.VMEM((NZ, 2, FL, ND), BF16),
-            pltpu.VMEM((2, NX, NP, 2, *unit), BF16),
+            pltpu.VMEM((2, NX, NP, 2, 2 * FD, QA), BF16),
+            pltpu.VMEM((2, NP, NX, 2 * FD, QB), BF16),
             pltpu.VMEM((E, NV), BF16),
             pltpu.VMEM((ND, E), BF16),
             pltpu.VMEM((E, ND), BF16),
@@ -683,16 +769,16 @@
             pltpu.VMEM((2, 2, *unit), BF16),
             pltpu.VMEM((3, 2, *unit), BF16),
             pltpu.VMEM((2, NZ, 2, FL, ND // 2), BF16),
-            pltpu.VMEM((2, 7, 2, FL, ND // 2), BF16),
-            pltpu.VMEM((2, 2, FL, ND // 2), BF16),
-            pltpu.VMEM((2, 2, FL, ND // 2), BF16),
+            pltpu.VMEM((2, 3, 2, FL, ND // 2), BF16),
+            pltpu.VMEM((2, 10, FL, ND // 2), BF16),
             pltpu.VMEM((1, NV), F32),
             dma, dma((2,)), dma, dma, dma((7, 2)), dma((7, 2)),
+            dma((3,)), dma((3,)), dma((2, 2)), dma((2, 2)), dma((2, 2)), dma((2, 2)), dma, dma,
             dma((2, 2)), dma((2, 2)), dma((2, 2)), dma((2, 2)), dma((NP, 2, 2)), dma((NP, 2, 2)), dma((NP, 2)), dma((NP, 2)), dma, dma,
             dma((2,)), dma((2,)), dma((2,)), dma((2,)), dma((2,)), dma((2,)),
             dma((4,)), dma((4,)), dma((NP, 2)), dma((NP, 2)), dma((2, NP, 2)), dma((2, NP, 2)),
             dma((2, 2)), dma((2, 2)), dma((2, 2)), dma((2, 2)),
-            dma((2, 7)), dma((2, 7)), dma((2,)), dma((2,)), dma((2, 2)),
+            dma((2, 3)), dma((2, 3)), dma((2,)), dma((2,)),
         ],
         compiler_params=pltpu.CompilerParams(
             collective_id=0, has_side_effects=True, vmem_limit_bytes=48 * 2**20

time: 103 us -> 94 us (0.913); the launches traced: 103 us -> 92.8 us
  Pallas kernels: 99.3 us -> 89.2 us
    pallas_call x1, Pallas kernels: 99.3 us -> 89.2 us  [body(): pl.pallas_call(kernel, out_shape=(jax.ShapeDtypeStruct((FL, ND), BF16), j...]
where the time goes in v4:
time: 94 us; the launch traced here: 92.8 us
  Pallas kernels  89.2 us (95%)
  local copies, waits for them, and re-layouts  2.95 us (3%)
    pallas_call x1, Pallas kernels, body(): pl.pallas_call(kernel, out_shape=(jax.ShapeDtypeStruct((FL, ND), BF16), j...  89.2 us
    unnamed x6, local copies, waits for them, and re-layouts  2.95 us

profile of v4, /device:TPU:1, one launch (start us, length us, event | category | flops | bytes accessed | tf_op | source)
XLA Modules:
  0.0 92.8 jit_solution(15893879077123704952)
XLA Ops:
  0.6 0.0 copy-start
  0.6 0.9 copy-done
  1.5 0.0 copy-start.1
  1.5 0.8 copy-done.1
  2.3 89.2 %shard_map.41 = (bf16[48,512]{1,0:T(8,128)(2,1)S(1)}, bf16[24,2048]{1,0:T(8,128)(2,1)S(1)}) custom-call(bf16[48,512]{1,0:T(8,128)(2,1)S(1)} %bitcast.7, bf16[24,2048]{1,0:T(8,128)(2,1)S(1)} %bitcast.6), custom_call_target="tpu_custom_call" | custom-call | flops 4831838208 | bytes 294912 | tf_op jit(solution)/shard_map/pallas_call | solution.py:742
  91.6 0.6 copy.6
  92.2 0.6 copy.7
Async XLA Ops:
  0.6 0.9 copy-start
  1.5 0.8 copy-start.1

commit v5 on v4

--- a/solution.py
+++ b/solution.py
@@ -28,7 +28,7 @@
 def kernel(
     docs_ref, cent_ref, res_ref, means_ref,
     own, gb, dg, cg, cgb, ct, xn, dt, kk, ww, ss, rr, ub, pbuf, ybuf, xbuf,
-    gs, og, rc, ra1, ra2, rf, rt, qq, sq, rp, vv,
+    wt, gs, og, rc, ra1, ra2, rf, rt, qq, sq, rp, vv,
     d1_send, d1_recv, d2_send, d2_recv, dz_send, dz_recv,
     bx_send, bx_recv, by_send, by_recv, bw_send, bw_recv, bc_send, bc_recv,
     cy_send, cy_recv, cw_send, cw_recv, cx_send, cx_recv, cf_send, cf_recv, cc_send, cc_recv,
@@ -366,14 +366,14 @@
             step_f(3, h)
 
     step_bw(1)
-    took(cg.at[0], cc_recv)
-    took(cgb.at[0], bc_recv)
-
     dt[...] = dg[...].reshape(E, ND)
     for j in range(4):
         block = dt[:, pl.ds(128 * j, 128)].astype(F32)
         scale = 1.0 / jnp.sqrt(jnp.sum(block * block, axis=0, keepdims=True) * (1.0 / E) + 1e-06)
         xn[pl.ds(128 * j, 128), :] = (block * scale).T.astype(BF16)
+
+    took(cg.at[0], cc_recv)
+    took(cgb.at[0], bc_recv)
 
     ss[...] = jnp.zeros_like(ss)
 
@@ -406,7 +406,7 @@
         rr[...] += k[:, 0:128] + k[:, 128:256]
         return 0
 
-    lax.fori_loop(0, NV // T, scores, 0)
+    lax.fori_loop(0, NV // T, scores, 0, unroll=4)
 
     def reduce_leaf(i):
         pbuf[i, mine_leaf] = jnp.sum(rr[...].T, axis=0, keepdims=True)
@@ -431,7 +431,7 @@
             xbuf[i, x, :, cols] = total
             return 0
 
-        lax.fori_loop(0, NV // 128, one, 0)
+        lax.fori_loop(0, NV // 128, one, 0, unroll=2)
 
     def send_x(i):
         def send(j, _):
@@ -468,7 +468,7 @@
         rr[...] += kk[:, cols] * vv[:, cols]
         return 0
 
-    lax.fori_loop(0, NV // 128, rows_of, 0)
+    lax.fori_loop(0, NV // 128, rows_of, 0, unroll=4)
     reduce_leaf(1)
     columns(1)
     send_x(1)
@@ -584,9 +584,14 @@
 
     H = ND // 2
 
-    def weigh(n, _):
-        cols = pl.ds(pl.multiple_of(n * 128, 128), 128)
-        ww[:, cols] = (kk[:, cols] * ub[...] * vv[:, cols]).astype(BF16)
+    def turn(n, _):
+        at = pl.ds(pl.multiple_of(n * 128, 128), 128)
+        wt[at, :] = ww[:, at].T
+        return 0
+
+    def weigh(t, _):
+        rows = pl.ds(pl.multiple_of(t * FL, FL), FL)
+        ct[rows, :] = (ct[rows, :].astype(F32) * vv[...]).astype(BF16)
         return 0
 
     def qz(h, i):
@@ -613,15 +618,11 @@
                 rp[h, 2 * (o + 2) + b] = qq[h, z, a]
 
     def recon(h):
-        part = lax.dot_general(
-            ct[...], ww[h * H:(h + 1) * H, :], (((1,), (1,)), ((), ())), preferred_element_type=F32
-        )
+        part = jnp.dot(ct[...], wt[:, h * H:(h + 1) * H], preferred_element_type=F32)
         for t in range(NL):
             qq[h, t // 2, t % 2] = part[FL * t:FL * t + FL].astype(BF16)
         for i in (2, 0, 1):
             qz(h, i).start()
-        for o in (1, -1, 0):
-            send_home(h, o)
 
     def step_q(h):
         for w, o in enumerate((2, -2)):
@@ -662,6 +663,7 @@
     products(3)
     across(2).wait_recv()
     step_plain(1)
+    lax.fori_loop(0, NV // 128, turn, 0, unroll=2)
     for n in ORDER:
         step_joined(n, 0)
         step_joined(n, 1)
@@ -669,17 +671,20 @@
     for i in range(4):
         across(i).wait_send()
     take_y(1)
-    lax.fori_loop(0, NV // 128, weigh, 0)
+    lax.fori_loop(0, NL, weigh, 0, unroll=2)
     recon(0)
+    recon(1)
+    for h in range(2):
+        for o in (1, -1, 0):
+            send_home(h, o)
     for h in range(2):
         step_home(2, h)
-    recon(1)
     for h in range(2):
         step_home(3, h)
     step_q(0)
+    step_q(1)
     step_home(0, 0)
     step_home(1, 0)
-    step_q(1)
     step_home(0, 1)
     step_home(1, 1)
 
@@ -761,6 +766,7 @@
             pltpu.VMEM((2, NL, 1, ND), F32),
             pltpu.VMEM((2, NY, 1, NV), F32),
             pltpu.VMEM((2, NX, 1, NV), F32),
+            pltpu.VMEM((NV, ND), BF16),
             pltpu.VMEM((192, NV), F32),
             pltpu.VMEM((2, NX, NP, 2, *unit), BF16),
             pltpu.VMEM((NX, NP, 2, *unit), BF16),

time: 94 us -> 92.4 us (0.983); the launches traced: 92.8 us -> 92.2 us
  no operation moved by 1% of the time
where the time goes in v5:
time: 92.4 us; the launch traced here: 92.2 us
  Pallas kernels  88.6 us (96%)
  local copies, waits for them, and re-layouts  2.95 us (3%)
    pallas_call x1, Pallas kernels, body(): pl.pallas_call(kernel, out_shape=(jax.ShapeDtypeStruct((FL, ND), BF16), j...  88.6 us
    unnamed x6, local copies, waits for them, and re-layouts  2.95 us

profile of v5, /device:TPU:1, one launch (start us, length us, event | category | flops | bytes accessed | tf_op | source)
XLA Modules:
  0.0 92.2 jit_solution(4907830584435879382)
XLA Ops:
  0.6 0.0 copy-start
  0.6 0.9 copy-done
  1.5 0.0 copy-start.1
  1.5 0.8 copy-done.1
  2.3 88.6 %shard_map.41 = (bf16[48,512]{1,0:T(8,128)(2,1)S(1)}, bf16[24,2048]{1,0:T(8,128)(2,1)S(1)}) custom-call(bf16[48,512]{1,0:T(8,128)(2,1)S(1)} %bitcast.7, bf16[24,2048]{1,0:T(8,128)(2,1)S(1)} %bitcast.6), custom_call_target="tpu_custom_call" | custom-call | flops 4831838208 | bytes 294912 | tf_op jit(solution)/shard_map/pallas_call | solution.py:747
  90.9 0.6 copy.6
  91.5 0.6 copy.7
Async XLA Ops:
  0.6 0.9 copy-start
  1.5 0.8 copy-start.1

commit v6 on v5

--- a/solution.py
+++ b/solution.py
@@ -28,7 +28,7 @@
 def kernel(
     docs_ref, cent_ref, res_ref, means_ref,
     own, gb, dg, cg, cgb, ct, xn, dt, kk, ww, ss, rr, ub, pbuf, ybuf, xbuf,
-    wt, gs, og, rc, ra1, ra2, rf, rt, qq, sq, rp, vv,
+    wt, cv, gs, og, rc, ra1, ra2, rf, rt, qq, sq, rp, vv,
     d1_send, d1_recv, d2_send, d2_recv, dz_send, dz_recv,
     bx_send, bx_recv, by_send, by_recv, bw_send, bw_recv, bc_send, bc_recv,
     cy_send, cy_recv, cw_send, cw_recv, cx_send, cx_recv, cf_send, cf_recv, cc_send, cc_recv,
@@ -589,11 +589,6 @@
         wt[at, :] = ww[:, at].T
         return 0
 
-    def weigh(t, _):
-        rows = pl.ds(pl.multiple_of(t * FL, FL), FL)
-        ct[rows, :] = (ct[rows, :].astype(F32) * vv[...]).astype(BF16)
-        return 0
-
     def qz(h, i):
         to, o = BACK[i] if i < 2 else LAST_BACK[h]
         return copy(
@@ -617,12 +612,17 @@
             def _():
                 rp[h, 2 * (o + 2) + b] = qq[h, z, a]
 
-    def recon(h):
-        part = jnp.dot(ct[...], wt[:, h * H:(h + 1) * H], preferred_element_type=F32)
-        for t in range(NL):
-            qq[h, t // 2, t % 2] = part[FL * t:FL * t + FL].astype(BF16)
-        for i in (2, 0, 1):
-            qz(h, i).start()
+    def recon(targets, at):
+        for i, o in enumerate(targets):
+            rows = pl.ds(pl.multiple_of(at_z(o) * 2 * FL, 2 * FL), 2 * FL)
+            r = at + 2 * FL * i
+            cv[r:r + 2 * FL, :] = (ct[rows, :].astype(F32) * vv[...]).astype(BF16)
+        part = jnp.dot(cv[at:at + 2 * FL * len(targets), :], wt[...], preferred_element_type=F32)
+        for i, o in enumerate(targets):
+            for e in range(2):
+                r = (2 * i + e) * FL
+                for h in range(2):
+                    qq[h, at_z(o), e] = part[r:r + FL, h * H:(h + 1) * H].astype(BF16)
 
     def step_q(h):
         for w, o in enumerate((2, -2)):
@@ -671,9 +671,11 @@
     for i in range(4):
         across(i).wait_send()
     take_y(1)
-    lax.fori_loop(0, NL, weigh, 0, unroll=2)
-    recon(0)
-    recon(1)
+    recon((4, 3, -3), 0)
+    for h in range(2):
+        for i in (2, 0, 1):
+            qz(h, i).start()
+    recon((2, -2, 1, -1, 0), 6 * FL)
     for h in range(2):
         for o in (1, -1, 0):
             send_home(h, o)
@@ -767,6 +769,7 @@
             pltpu.VMEM((2, NY, 1, NV), F32),
             pltpu.VMEM((2, NX, 1, NV), F32),
             pltpu.VMEM((NV, ND), BF16),
+            pltpu.VMEM((E, NV), BF16),
             pltpu.VMEM((192, NV), F32),
             pltpu.VMEM((2, NX, NP, 2, *unit), BF16),
             pltpu.VMEM((NX, NP, 2, *unit), BF16),

time: 92.4 us -> 89.4 us (0.968)
  Pallas kernels: 88.6 us -> 85.6 us
    pallas_call x1, Pallas kernels: 88.6 us -> 85.6 us  [body(): pl.pallas_call(kernel, out_shape=(jax.ShapeDtypeStruct((FL, ND), BF16), j...]
where the time goes in v6:
time: 89.4 us; the launch traced here: 89.2 us
  Pallas kernels  85.6 us (96%)
  local copies, waits for them, and re-layouts  2.95 us (3%)
    pallas_call x1, Pallas kernels, body(): pl.pallas_call(kernel, out_shape=(jax.ShapeDtypeStruct((FL, ND), BF16), j...  85.6 us
    unnamed x6, local copies, waits for them, and re-layouts  2.95 us

profile of v6, /device:TPU:1, one launch (start us, length us, event | category | flops | bytes accessed | tf_op | source)
XLA Modules:
  0.0 89.2 jit_solution(11538909006577233633)
XLA Ops:
  0.6 0.0 copy-start
  0.6 0.9 copy-done
  1.5 0.0 copy-start.1
  1.5 0.8 copy-done.1
  2.3 85.6 %shard_map.41 = (bf16[48,512]{1,0:T(8,128)(2,1)S(1)}, bf16[24,2048]{1,0:T(8,128)(2,1)S(1)}) custom-call(bf16[48,512]{1,0:T(8,128)(2,1)S(1)} %bitcast.7, bf16[24,2048]{1,0:T(8,128)(2,1)S(1)} %bitcast.6), custom_call_target="tpu_custom_call" | custom-call | flops 4831838208 | bytes 294912 | tf_op jit(solution)/shard_map/pallas_call | solution.py:749
  88.0 0.6 copy.6
  88.6 0.6 copy.7
Async XLA Ops:
  0.6 0.9 %copy-start = (bf16[2048,24]{0,1:T(8,128)(2,1)S(1)}, bf16[2048,24]{0,1:T(8,128)(2,1)}, u32[]{:S(2)}) copy-start(bf16[2048,24]{0,1:T(8,128)(2,1)} %param.3) | copy-start | bytes 294916
  1.5 0.8 copy-start.1

commit v7 on v6

--- a/solution.py
+++ b/solution.py
@@ -658,13 +658,13 @@
     step_first()
     products(2)
     send_y(1)
+    lax.fori_loop(0, NV // 128, turn, 0, unroll=2)
     across(1).wait_recv()
     step_plain(0)
     products(3)
     across(2).wait_recv()
     step_plain(1)
-    lax.fori_loop(0, NV // 128, turn, 0, unroll=2)
-    for n in ORDER:
+    for n in (2, 3):
         step_joined(n, 0)
         step_joined(n, 1)
     across(3).wait_recv()
@@ -675,6 +675,9 @@
     for h in range(2):
         for i in (2, 0, 1):
             qz(h, i).start()
+    for n in (0, 1):
+        step_joined(n, 0)
+        step_joined(n, 1)
     recon((2, -2, 1, -1, 0), 6 * FL)
     for h in range(2):
         for o in (1, -1, 0):

time: 89.4 us -> 89.9 us (level)
  no operation moved by 1% of the time
where the time goes in v7:
time: 89.9 us; the launch traced here: 89.7 us
  Pallas kernels  86.1 us (96%)
  local copies, waits for them, and re-layouts  2.95 us (3%)
    pallas_call x1, Pallas kernels, body(): pl.pallas_call(kernel, out_shape=(jax.ShapeDtypeStruct((FL, ND), BF16), j...  86.1 us
    unnamed x6, local copies, waits for them, and re-layouts  2.95 us

profile of v7, /device:TPU:1, one launch (start us, length us, event | category | flops | bytes accessed | tf_op | source)
XLA Modules:
  0.0 89.7 jit_solution(9979413085966992726)
XLA Ops:
  0.6 0.0 copy-start
  0.6 0.9 copy-done
  1.5 0.0 copy-start.1
  1.5 0.8 copy-done.1
  2.3 86.1 %shard_map.41 = (bf16[48,512]{1,0:T(8,128)(2,1)S(1)}, bf16[24,2048]{1,0:T(8,128)(2,1)S(1)}) custom-call(bf16[48,512]{1,0:T(8,128)(2,1)S(1)} %bitcast.7, bf16[24,2048]{1,0:T(8,128)(2,1)S(1)} %bitcast.6), custom_call_target="tpu_custom_call" | custom-call | flops 4831838208 | bytes 294912 | tf_op jit(solution)/shard_map/pallas_call | solution.py:752
  88.4 0.6 copy.6
  89.0 0.6 copy.7
Async XLA Ops:
  0.6 0.9 copy-start
  1.5 0.8 copy-start.1
